TPU v7x, 128 devices: a whole 4x4x4 slice. The times are simulated.
128 devices in a mesh: seq: 4 (over x), ctx: 16 (over y_hi, z, core), exp: 2 (over y_lo).
Axes of the slice: x: 4, y: 4 (y_hi: 2, y_lo: 2; y = y_hi * 2 + y_lo), z: 4, core: 2. Of those that a mesh axis runs over, the one named last changes fastest.
Arguments:
- tokens: bfloat16 [8, 2048, 768], P(('seq', 'exp'), 'ctx'), may hold values from -6 to 6
- cotangent: bfloat16 [8, 2048, 768], P(('seq', 'exp'), 'ctx'), may hold values from -6 to 6
- routes: int32 [8, 2048, 2], P(('seq', 'exp'), 'ctx'), may hold values from 0 to 63, all different within a row; in each aligned block of 128 rows (0 to 127, 128 to 255, ..., all dimensions but the last counted through in order) at most 8 rows name the same one
- w_query: bfloat16 [768, 768], P(('seq', 'ctx', 'exp')), may hold values from -0.21875 to 0.21875
- w_key: bfloat16 [768, 768], P(('seq', 'ctx', 'exp')), may hold values from -0.21875 to 0.21875
- w_value: bfloat16 [768, 768], P(('seq', 'ctx', 'exp')), may hold values from -0.21875 to 0.21875
- w_output: bfloat16 [768, 768], P(('seq', 'ctx', 'exp')), may hold values from -4 to 4
- w_router: bfloat16 [768, 64], P(('seq', 'ctx', 'exp')), may hold values from -0.15625 to 0.15625
- gain_attn: bfloat16 [768], P(('seq', 'ctx', 'exp')), may hold values from 0.5 to 1.5
- gain_ffn: bfloat16 [768], P(('seq', 'ctx', 'exp')), may hold values from 0.5 to 1.5
- bias_table: float32 [32, 12], replicated, may hold values from -3 to 3
- w_in: bfloat16 [64, 768, 3072], P(('seq', 'ctx'), None, 'exp'), may hold values from -0.21875 to 0.21875
- w_out: bfloat16 [64, 3072, 768], P(('seq', 'ctx'), 'exp'), may hold values from -0.21875 to 0.21875
Outputs:
- out: bfloat16 [8, 2048, 768], P(('seq', 'exp'), 'ctx')
- grad_tokens: float32 [8, 2048, 768], P(('seq', 'exp'), 'ctx')
- grad_query: float32 [768, 768], P(('seq', 'ctx', 'exp'))
- grad_key: float32 [768, 768], P(('seq', 'ctx', 'exp'))
- grad_value: float32 [768, 768], P(('seq', 'ctx', 'exp'))
- grad_output: float32 [768, 768], P(('seq', 'ctx', 'exp'))
- grad_router: float32 [768, 64], P(('seq', 'ctx', 'exp'))
- grad_gain_attn: float32 [768], P(('seq', 'ctx', 'exp'))
- grad_gain_ffn: float32 [768], P(('seq', 'ctx', 'exp'))
- grad_table: float32 [32, 12], replicated
- grad_in: float32 [64, 768, 3072], P(('seq', 'ctx'), None, 'exp')
- grad_out: float32 [64, 3072, 768], P(('seq', 'ctx'), 'exp')
Inputs may be any that keep to these rules, and one draw needn't show every extreme that they name: `routes`: each row names 2 different experts. Within each aligned block of 128 rows of a sequence (the rows of one device) no expert is named more than 8 times, a bound that some block reaches.
All inputs are finite; a program needn't handle non-finite values.
Results may differ from a plain program's by a relative error of at most 0.02.
Values may be sent and summed in bfloat16 or wider, within the bound.
No kernel may reach another device: no remote copies, remote signals or barrier semaphores. Data moves between devices by JAX's collectives and lax.ppermute only.
A program may use at most 192 MiB of HBM per device.

v0:
```python
import functools
import math

import jax
import jax.numpy as jnp
import numpy as np
from jax import lax
from jax.experimental import pallas as pl
from jax.experimental.pallas import tpu as pltpu
from jax.sharding import Mesh
from jax.sharding import PartitionSpec as P

HEADS = 12
HEAD = 64
TOP = 2
BUCKETS = 32
MAXDIST = 128
WIDTH = HEADS * HEAD
HALF = WIDTH // 2
PAIRS = HALF // 128
SIDE_GAIN = 64
SIDE_END = WIDTH + 128
FAR_LANE = 2 * 128 - 127
EXPERT_BLOCK = 256
EXPERT_VMEM = 60 * 2**20
TILE = 128
CHUNK = 256
CORE = "ctx_2"
CHIPS = ("ctx_0", "ctx_1")
SAME_CORE = ("exp", "seq", "ctx_0", "ctx_1")
QUAD = ("ctx_2", "exp")
SEQ_CTX_EXP = ("seq", "ctx_0", "ctx_1", "ctx_2", "exp")
CTX = ("ctx_0", "ctx_1", "ctx_2")
SEQ_CTX = ("seq", "ctx_0", "ctx_1", "ctx_2")
BLOCKED = -1000000000.0
epsilon = 1e-06
precise = lax.Precision.HIGHEST


def limits():
    exact_cut = BUCKETS // 2
    borders = []
    for bucket_step in range(1, BUCKETS):
        if bucket_step <= exact_cut:
            borders.append(bucket_step)
        else:
            borders.append(
                int(
                    math.ceil(
                        exact_cut * (MAXDIST / exact_cut) ** ((bucket_step - exact_cut) / exact_cut)
                    )
                )
            )
    return borders


def rows_dot(first_op, second_op):
    return lax.dot_general(
        first_op, second_op, (((0,), (0,)), ((), ())), preferred_element_type=jnp.float32
    )


def cols_dot(first_op, second_op):
    return lax.dot_general(
        first_op, second_op, (((1,), (1,)), ((), ())), preferred_element_type=jnp.float32
    )


def plain_dot(first_op, second_op):
    return jnp.dot(first_op, second_op, preferred_element_type=jnp.float32)


def own_tiles(place_ref):
    first = place_ref[0]
    return first, 15 - first


def fill_bias(bias_full, place_ref):
    tile_a, tile_b = own_tiles(place_ref)

    def fill(tile, carry):
        at = pl.ds(pl.multiple_of(tile * TILE, TILE), TILE)
        bias_full[0:256, at] = jnp.full((256, TILE), jnp.where(tile <= tile_a, 0.0, BLOCKED))
        bias_full[256:512, at] = jnp.full((256, TILE), jnp.where(tile <= tile_b, 0.0, BLOCKED))
        return carry

    lax.fori_loop(0, 16, fill, 0)


def near_kernel(table_ref, near_ref):
    row = lax.broadcasted_iota(jnp.int32, (TILE, 2 * TILE), 0)
    column = lax.broadcasted_iota(jnp.int32, (TILE, 2 * TILE), 1)
    distance = row + TILE - column
    for head in range(2 * PAIRS):
        last = table_ref[BUCKETS - 1, head]
        bias = jnp.full(distance.shape, table_ref[0, head] - last)
        for bucket, border in enumerate(limits()):
            bias = jnp.where(distance >= border, table_ref[bucket + 1, head] - last, bias)
        rows = slice(TILE * (head % 2), TILE * (head % 2) + TILE)
        near_ref[head // 2, rows, :] = jnp.where(distance >= 0, bias, BLOCKED)


def near_bias(bias_full, near_ref, place_ref, pair):
    tile_a, tile_b = own_tiles(place_ref)
    for rows, tile in ((slice(0, 256), tile_a), (slice(256, 512), tile_b)):
        bias_full[rows, pl.ds(pl.multiple_of(tile * TILE, TILE), TILE)] = near_ref[pair, :, TILE:]

        @pl.when(tile > 0)
        def _():
            before = pl.ds(pl.multiple_of((tile - 1) * TILE, TILE), TILE)
            bias_full[rows, before] = near_ref[pair, :, :TILE]


def by_head(rows):
    left = lax.broadcasted_iota(jnp.int32, (TILE, TILE), 1) < HEAD
    rows = rows.astype(jnp.float32)
    parts = []
    for tile in (rows[:TILE], rows[TILE:]):
        parts.append(jnp.where(left, tile, 0.0))
        parts.append(jnp.where(left, 0.0, tile))
    return jnp.concatenate(parts, axis=0)


def side_by_side(four):
    left = lax.broadcasted_iota(jnp.int32, (TILE, TILE), 1) < HEAD
    return (
        jnp.where(left, four[:TILE], four[TILE : 2 * TILE]),
        jnp.where(left, four[2 * TILE : 3 * TILE], four[3 * TILE :]),
    )


def later_units(tile_a):
    reach = tile_a // 2
    units = []
    for step in range(1, 4):
        of_first = step <= reach
        chunk = jnp.where(of_first, step, 4 + step - reach)
        units.append((of_first, jnp.where(of_first, 0, 256), chunk))
    return units


def chunk_at(chunk):
    return pl.ds(pl.multiple_of(chunk * CHUNK, CHUNK), CHUNK)


def row_at(first):
    return pl.ds(pl.multiple_of(first, 256), 256)


def pair_lanes(pair):
    return pl.ds(pl.multiple_of(pair * 128, 128), 128)


def side_row(side, lane):
    return jnp.concatenate(
        [
            jnp.transpose(side[128 * step : 128 * step + 128].astype(jnp.float32))[lane : lane + 1]
            for step in range(WIDTH // 128)
        ],
        axis=1,
    )


def attend_kernel(
    place_ref,
    mine_any,
    other_any,
    weights_any,
    near_any,
    normed_any,
    k_any,
    v_any,
    q_ref,
    att_ref,
    lse_ref,
    side_ref,
    bias_full,
    scores,
    query,
    tokens,
    weights_ref,
    near_ref,
    normed_ref,
    k_ref,
    v_ref,
    sems,
):
    load_first = pltpu.make_async_copy(weights_any.at[0], weights_ref.at[0], sems.at[0])
    load_second = pltpu.make_async_copy(weights_any.at[1], weights_ref.at[1], sems.at[1])
    load_near = pltpu.make_async_copy(near_any, near_ref, sems.at[4])
    save_normed = pltpu.make_async_copy(normed_ref, normed_any, sems.at[5])
    save_k = pltpu.make_async_copy(k_ref, k_any, sems.at[6])
    save_v = pltpu.make_async_copy(v_ref, v_any, sems.at[7])
    tile_a, tile_b = own_tiles(place_ref)
    core = place_ref[1]

    def load_tokens(block):
        slab = block if block < 16 else 31 - block
        chip, row = slab // 2, 0 if block < 16 else 64
        copies = []
        for which, (from_any, from_core) in enumerate(((mine_any, core), (other_any, 1 - core))):
            to_block = 2 * chip + from_core if block < 16 else 31 - 2 * chip - from_core
            copies.append(
                pltpu.make_async_copy(
                    from_any.at[chip, row : row + 64],
                    tokens.at[pl.ds(pl.multiple_of(to_block * 64, 64), 64)],
                    sems.at[8 + block // 2 * 2 + which],
                )
            )
        return copies

    load_first.start()
    for block in range(0, 8, 2):
        for copy in load_tokens(block):
            copy.start()
    load_second.start()
    for block in range(8, 32, 2):
        for copy in load_tokens(block):
            copy.start()
    load_near.start()
    fill_bias(bias_full, place_ref)
    load_first.wait()
    side_ref[...] = weights_ref[0, :, WIDTH:]
    gain = side_row(side_ref[...], SIDE_GAIN)

    def norm_part(part):
        for block in range(8 * part, 8 * part + 8, 2):
            for copy in load_tokens(block):
                copy.wait()
            at = slice(64 * block, 64 * block + 128)
            source = tokens[at, :].astype(jnp.float32)
            inv = lax.rsqrt(jnp.mean(source * source, axis=-1, keepdims=True) + epsilon)
            normed_ref[at, :] = (source * inv * gain).astype(jnp.bfloat16)

    norm_part(0)
    load_second.wait()
    for part in range(4):
        if part < 3:
            norm_part(part + 1)
        at = slice(512 * part, 512 * part + 512)
        rows = normed_ref[at, :]
        for to_ref, weight in (
            (k_ref, weights_ref[0, :, HALF:WIDTH]),
            (v_ref, weights_ref[1, :, :HALF]),
        ):
            product = plain_dot(rows, weight).astype(jnp.bfloat16)
            for pair in range(PAIRS):
                to_ref[pair, at, :] = product[:, 128 * pair : 128 * pair + 128]
    save_normed.start()
    save_k.start()
    save_v.start()
    own = jnp.concatenate(
        [
            normed_ref[pl.ds(pl.multiple_of(tile_a * TILE, TILE), TILE), :],
            normed_ref[pl.ds(pl.multiple_of(tile_b * TILE, TILE), TILE), :],
        ],
        axis=0,
    )
    q_ref[...] = plain_dot(own, weights_ref[0, :, :HALF]).astype(jnp.bfloat16)
    load_near.wait()
    units = later_units(tile_a)
    lse_ref[...] = jnp.zeros_like(lse_ref)

    def one_pair(pair, carry):
        near_bias(bias_full, near_ref, place_ref, pair)
        lanes = pair_lanes(pair)
        query[...] = (by_head(q_ref[:, lanes]) * HEAD**-0.5).astype(jnp.bfloat16)

        def widest(part):
            return jnp.maximum(part[:, :128], part[:, 128:])

        both = cols_dot(query[...], k_ref[pair, 0:CHUNK, :]) + bias_full[:, 0:CHUNK]
        scores[0], scores[4] = both[:256], both[256:]
        top_a, top_b = widest(both[:256]), widest(both[256:])
        for chunk in range(1, 5):
            at = slice(chunk * CHUNK, (chunk + 1) * CHUNK)
            part = cols_dot(query[256:512, :], k_ref[pair, at, :]) + bias_full[256:512, at]
            scores[4 + chunk] = part
            top_b = jnp.maximum(top_b, widest(part))
        for step, (of_first, first, chunk) in enumerate(units):
            part = (
                cols_dot(query[row_at(first), :], k_ref[pair, chunk_at(chunk), :])
                + bias_full[row_at(first), chunk_at(chunk)]
            )
            scores[1 + step] = part
            here = widest(part)
            top_a = jnp.maximum(top_a, jnp.where(of_first, here, 2 * BLOCKED))
            top_b = jnp.maximum(top_b, jnp.where(of_first, 2 * BLOCKED, here))
        top_a = jnp.max(top_a, axis=-1, keepdims=True)
        top_b = jnp.max(top_b, axis=-1, keepdims=True)

        def raise_to(part, top, at):
            raised = jnp.exp(part - top)
            return raised[:, :128] + raised[:, 128:], plain_dot(
                raised.astype(jnp.bfloat16), v_ref[pair, at, :]
            )

        total_a, merged_a = raise_to(scores[0], top_a, slice(0, CHUNK))
        total_b, merged_b = raise_to(scores[4], top_b, slice(0, CHUNK))
        for chunk in range(1, 5):
            here, product = raise_to(
                scores[4 + chunk], top_b, slice(chunk * CHUNK, (chunk + 1) * CHUNK)
            )
            total_b, merged_b = total_b + here, merged_b + product
        for step, (of_first, first, chunk) in enumerate(units):
            top = jnp.where(of_first, top_a, top_b)
            here, product = raise_to(scores[1 + step], top, chunk_at(chunk))
            total_a = total_a + jnp.where(of_first, here, 0.0)
            total_b = total_b + jnp.where(of_first, 0.0, here)
            merged_a = merged_a + jnp.where(of_first, product, 0.0)
            merged_b = merged_b + jnp.where(of_first, 0.0, product)
        total_a = jnp.sum(total_a, axis=-1, keepdims=True)
        total_b = jnp.sum(total_b, axis=-1, keepdims=True)
        lane = lax.broadcasted_iota(jnp.int32, (2 * TILE, 128), 1)
        for rows, lse in (
            (slice(0, 256), top_a + jnp.log(total_a)),
            (slice(256, 512), top_b + jnp.log(total_b)),
        ):
            lse_ref[rows, :] = jnp.where(lane == pair, lse, lse_ref[rows, :])
        first, second = side_by_side(
            jnp.concatenate([merged_a / total_a, merged_b / total_b], axis=0)
        )
        first, second = first.astype(jnp.bfloat16), second.astype(jnp.bfloat16)
        att_ref[0, 0:64, lanes] = first[:64]
        att_ref[1, 0:64, lanes] = first[64:]
        att_ref[1, 64:128, lanes] = second[:64]
        att_ref[0, 64:128, lanes] = second[64:]
        return carry

    lax.fori_loop(0, PAIRS, one_pair, 0)
    save_normed.wait()
    save_k.wait()
    save_v.wait()


def core_rows(core):
    return pl.ds(pl.multiple_of(core * HALF, 128), HALF)


def mid_kernel(
    place_ref,
    mine_ref,
    other_ref,
    tokens_ref,
    side_ref,
    wo_mine_ref,
    wo_other_ref,
    pack_ref,
    hidden_ref,
    normed_ref,
    packed_ref,
):
    core = place_ref[1]
    mine, other = mine_ref[core], other_ref[core]
    mine_rows, other_rows = core_rows(core), core_rows(1 - core)
    hidden_ref[:, mine_rows] = plain_dot(
        mine, wo_mine_ref[mine_rows, :]
    ) + plain_dot(other, wo_mine_ref[other_rows, :])
    hidden_ref[:, other_rows] = plain_dot(mine, wo_other_ref[mine_rows, :]) + plain_dot(
        other, wo_other_ref[other_rows, :]
    )
    hidden = tokens_ref[...].astype(jnp.float32) + hidden_ref[...]
    hidden_ref[...] = hidden
    inv = lax.rsqrt(jnp.mean(hidden * hidden, axis=-1, keepdims=True) + epsilon)
    normed = (hidden * inv * side_row(side_ref[...], SIDE_GAIN + 1)).astype(jnp.bfloat16)
    normed_ref[...] = normed
    packed_ref[...] = plain_dot(pack_ref[...], normed).astype(jnp.bfloat16)


def token_kernel(
    back_ref,
    pick_ref,
    hidden_ref,
    normed_ref,
    cot_ref,
    routes_ref,
    side_ref,
    out_ref,
    d_hidden_ref,
    d_mixed_ref,
    sums_ref,
):
    picked = plain_dot(pick_ref[...], back_ref[...])
    side = side_ref[...]
    logits = plain_dot(normed_ref[...], side)
    lane = lax.broadcasted_iota(jnp.int32, (TILE, 128), 1)
    routes = routes_ref[...]
    marks = [lane == routes[:, k : k + 1] for k in range(TOP)]
    chosen = [jnp.sum(jnp.where(mark, logits, 0.0), axis=-1, keepdims=True) for mark in marks]
    top = jnp.maximum(*chosen)
    raised = [jnp.exp(one - top) for one in chosen]
    gates = [one / (raised[0] + raised[1]) for one in raised]
    rows = [
        picked[TILE * k : TILE * k + TILE, :WIDTH].astype(jnp.bfloat16).astype(jnp.float32)
        for k in range(TOP)
    ]
    hidden = hidden_ref[...]
    out_ref[...] = (hidden + (gates[0] * rows[0] + gates[1] * rows[1])).astype(jnp.bfloat16)
    grad_top = cot_ref[...].astype(jnp.float32)
    d_gates = [jnp.sum(grad_top * one, axis=-1, keepdims=True) for one in rows]
    mean_gate = gates[0] * d_gates[0] + gates[1] * d_gates[1]
    d_logits = sum(
        jnp.where(mark, gate * (d_gate - mean_gate), 0.0)
        for mark, gate, d_gate in zip(marks, gates, d_gates)
    ).astype(jnp.bfloat16)
    d_normed = picked[:TILE, WIDTH:] + picked[TILE:, WIDTH:] + cols_dot(d_logits, side)
    inv = lax.rsqrt(jnp.mean(hidden * hidden, axis=-1, keepdims=True) + epsilon)
    scaled = side_row(side, SIDE_GAIN + 1) * d_normed
    d_hidden = (
        grad_top
        + inv * scaled
        - hidden * (inv * inv * inv) * jnp.mean(scaled * hidden, axis=-1, keepdims=True)
    )
    d_hidden_ref[...] = d_hidden
    d_mixed_ref[...] = d_hidden.astype(jnp.bfloat16)
    d_gain = jnp.sum(d_normed * hidden * inv, axis=0, keepdims=True)
    d_router = rows_dot(normed_ref[...], d_logits)
    for step in range(WIDTH // 128):
        at = slice(128 * step, 128 * step + 128)
        column = jnp.transpose(jnp.broadcast_to(d_gain[:, at], (128, 128)))
        sums_ref[at, :] = jnp.where(lane == SIDE_GAIN, column, d_router[at]).astype(jnp.bfloat16)


def tile_order(ref, lanes):
    return jnp.concatenate(
        [ref[0, 0:64, lanes], ref[1, 0:64, lanes], ref[1, 64:128, lanes], ref[0, 64:128, lanes]],
        axis=0,
    )


def by_distance(tiles):
    for half in (64, 32, 16, 8):
        tiles = tiles[:half] + pltpu.roll(tiles[half:], 2 * TILE - half, 1)
    row = lax.broadcasted_iota(jnp.int32, tiles.shape, 0)
    for step in (4, 2, 1):
        moved = pltpu.roll(tiles, 2 * TILE - step, 1)
        tiles = jnp.where((row & step) != 0, moved, tiles)
    return jnp.sum(tiles, axis=0, keepdims=True)


def wide(ref):
    return jnp.concatenate([ref[pair] for pair in range(PAIRS)], axis=1)


def back_kernel(
    place_ref,
    q_ref,
    k_any,
    v_any,
    att_ref,
    mixed_ref,
    mixed_other_ref,
    lse_ref,
    near_any,
    normed_t_any,
    att_t_any,
    side_ref,
    wo_mine_ref,
    wo_other_ref,
    dk_any,
    dv_any,
    sums_any,
    dq_ref,
    bias_full,
    d_scores,
    profile,
    d_mixed,
    d_att,
    query,
    grads,
    row_dots,
    row_lse,
    query_t,
    grads_t,
    dk_t,
    dv_t,
    k_ref,
    v_ref,
    near_ref,
    normed_t_ref,
    att_t_ref,
    dk_ref,
    dv_ref,
    sums_ref,
    sems,
):
    load_normed = pltpu.make_async_copy(normed_t_any, normed_t_ref, sems.at[0])
    load_att = pltpu.make_async_copy(att_t_any, att_t_ref, sems.at[1])
    def saves_of(pair):
        return [
            pltpu.make_async_copy(dk_ref.at[pair], dk_any.at[pair], sems.at[20 + 2 * pair]),
            pltpu.make_async_copy(dv_ref.at[pair], dv_any.at[pair], sems.at[21 + 2 * pair]),
        ]

    def loads_of(pair):
        return [
            pltpu.make_async_copy(from_any.at[pair], to_ref.at[pair], sems.at[8 + 4 * step + pair])
            for step, (from_any, to_ref) in enumerate(
                ((k_any, k_ref), (v_any, v_ref), (near_any, near_ref))
            )
        ]

    saves = [
        pltpu.make_async_copy(sums_ref.at[part], sums_any.at[part], sems.at[4 + part])
        for part in range(2)
    ]
    for pair in range(PAIRS):
        for load in loads_of(pair):
            load.start()
    load_normed.start()
    load_att.start()
    tile_a, tile_b = own_tiles(place_ref)
    core = place_ref[1]
    fill_bias(bias_full, place_ref)
    d_mixed[core] = mixed_ref[...]
    d_mixed[1 - core] = mixed_other_ref[...]
    d_att[...] = (
        cols_dot(tile_order(d_mixed, core_rows(core)), wo_mine_ref[core_rows(core), :])
        + cols_dot(tile_order(d_mixed, core_rows(1 - core)), wo_other_ref[core_rows(core), :])
    ).astype(jnp.bfloat16)
    units = later_units(tile_a)
    reach = tile_a // 2

    def one_pair(pair, carry):
        for load in loads_of(pair):
            load.wait()
        near_bias(bias_full, near_ref, place_ref, pair)
        lanes = pair_lanes(pair)
        query[...] = (by_head(q_ref[:, lanes]) * HEAD**-0.5).astype(jnp.bfloat16)
        some = by_head(d_att[:, lanes])
        outs = by_head(tile_order(att_ref, lanes))
        row_dots[...] = jnp.sum(some * outs, axis=-1, keepdims=True)
        grads[...] = some.astype(jnp.bfloat16)
        lane = lax.broadcasted_iota(jnp.int32, (4 * TILE, 128), 1)
        row_lse[...] = jnp.sum(jnp.where(lane == pair, lse_ref[...], 0.0), axis=-1, keepdims=True)
        rest = slice(5 * CHUNK, 8 * CHUNK)
        dk_t[:, rest] = jnp.zeros((128, 3 * CHUNK), jnp.float32)
        dv_t[:, rest] = jnp.zeros((128, 3 * CHUNK), jnp.float32)
        query_t[...] = jnp.transpose(query[...])
        grads_t[...] = jnp.transpose(grads[...])

        def unit(rows, at):
            keys = k_ref[pair, at, :]
            probs = jnp.exp(
                cols_dot(query[rows, :], keys) + bias_full[rows, at] - row_lse[rows, :]
            )
            d_part = probs * (cols_dot(grads[rows, :], v_ref[pair, at, :]) - row_dots[rows, :])
            low = d_part.astype(jnp.bfloat16)
            d_values = plain_dot(grads_t[:, rows], probs.astype(jnp.bfloat16))
            d_keys = plain_dot(query_t[:, rows], low)
            return d_part, plain_dot(low, keys), d_keys, d_values

        both, dq, d_keys, d_values = unit(slice(0, 512), slice(0, CHUNK))
        d_scores[0], d_scores[4] = both[:256], both[256:]
        dk_t[:, 0:CHUNK] = d_keys
        dv_t[:, 0:CHUNK] = d_values
        dq_a, dq_b = dq[:256], dq[256:]
        total = (both[:256, :128] + both[:256, 128:]) + (both[256:, :128] + both[256:, 128:])
        for chunk in range(1, 5):
            at = slice(chunk * CHUNK, (chunk + 1) * CHUNK)
            part, dq, d_keys, d_values = unit(slice(256, 512), at)
            d_scores[4 + chunk] = part
            dk_t[:, at] = d_keys
            dv_t[:, at] = d_values
            dq_b = dq_b + dq
            total = total + (part[:, :128] + part[:, 128:])
        for step, (of_first, first, chunk) in enumerate(units):
            at = chunk_at(chunk)
            part, dq, d_keys, d_values = unit(row_at(first), at)
            d_scores[1 + step] = part
            dk_t[:, at] = dk_t[:, at] + d_keys
            dv_t[:, at] = dv_t[:, at] + d_values
            dq_a = dq_a + jnp.where(of_first, dq, 0.0)
            dq_b = dq_b + jnp.where(of_first, 0.0, dq)
            total = total + (part[:, :128] + part[:, 128:])
        dk_ref[pair] = jnp.transpose(dk_t[...].astype(jnp.bfloat16))
        dv_ref[pair] = jnp.transpose(dv_t[...].astype(jnp.bfloat16))
        for copy in saves_of(pair):
            copy.start()
        first, second = side_by_side(jnp.concatenate([dq_a, dq_b], axis=0) * HEAD**-0.5)
        dq_ref[0:128, lanes] = first.astype(jnp.bfloat16)
        dq_ref[128:256, lanes] = second.astype(jnp.bfloat16)

        def tile_of(slot, tile):
            return d_scores[slot, :, pl.ds(pl.multiple_of(tile % 2 * TILE, TILE), TILE)]

        def slot_b(tile):
            chunk = tile // 2
            return jnp.where(chunk <= 4, 4 + chunk, chunk - 4 + reach)

        own = tile_of(reach, tile_a) + tile_of(slot_b(tile_b), tile_b)
        ahead = jnp.maximum(tile_a - 1, 0)
        before = tile_of(slot_b(tile_b - 1), tile_b - 1) + jnp.where(
            tile_a > 0, tile_of(ahead // 2, ahead), 0.0
        )
        far = total - own - before
        for head in range(2):
            rows = slice(TILE * head, TILE * head + TILE)
            sums = by_distance(jnp.concatenate([before[rows], own[rows]], axis=1))
            others = jnp.sum(far[rows], keepdims=True)
            lane = lax.broadcasted_iota(jnp.int32, (1, 2 * TILE), 1)
            sums = sums + jnp.where(lane == FAR_LANE, others, 0.0)
            high = sums.astype(jnp.bfloat16).astype(jnp.float32)
            for step, part in enumerate((high, sums - high)):
                for half in range(2):
                    cell = part[:, TILE * half : TILE * half + TILE]
                    row = 4 * (2 * pair + head) + 2 * step + half
                    profile[pl.ds(row, 1), :] = cell
                    profile[pl.ds(row + 24, 1), :] = cell
        return carry

    lax.fori_loop(0, PAIRS, one_pair, 0)
    load_normed.wait()
    load_att.wait()
    pair_mixed = jnp.concatenate([d_mixed[0, :, core_rows(core)], d_mixed[1, :, core_rows(core)]])
    sums_ref[1, :, HALF:WIDTH] = plain_dot(att_t_ref[...], pair_mixed).astype(jnp.bfloat16)
    sums_ref[1, :, :HALF] = plain_dot(normed_t_ref[...], wide(dv_ref)).astype(jnp.bfloat16)
    cells = profile[...].astype(jnp.bfloat16)
    for step in range(WIDTH // 48):
        sums_ref[1, 48 * step : 48 * step + 48, WIDTH:] = cells
    saves[1].start()
    own_t = jnp.concatenate(
        [
            normed_t_ref[:, pl.ds(pl.multiple_of(tile_a * TILE, TILE), TILE)],
            normed_t_ref[:, pl.ds(pl.multiple_of(tile_b * TILE, TILE), TILE)],
        ],
        axis=1,
    )
    sums_ref[0, :, :HALF] = plain_dot(own_t, dq_ref[...]).astype(jnp.bfloat16)
    sums_ref[0, :, HALF:WIDTH] = plain_dot(normed_t_ref[...], wide(dk_ref)).astype(jnp.bfloat16)
    sums_ref[0, :, WIDTH:] = side_ref[...]
    saves[0].start()
    for pair in range(PAIRS):
        for copy in saves_of(pair):
            copy.wait()
    saves[1].wait()
    saves[0].wait()


def spread_kernel(
    place_ref,
    dq_ref,
    dk_any,
    dv_any,
    weights_any,
    kept_any,
    given_any,
    dk_ref,
    dv_ref,
    weights_ref,
    rows_ref,
    sems,
):
    tile_a, tile_b = own_tiles(place_ref)
    core = place_ref[1]
    chunks = 4
    size = ROWS // chunks
    loads = [
        pltpu.make_async_copy(weights_any.at[part], weights_ref.at[part], sems.at[part])
        for part in range(2)
    ]
    for chunk in range(chunks):
        at = pl.ds(size * chunk, size)
        for step, (from_any, to_ref) in enumerate(((dk_any, dk_ref), (dv_any, dv_ref))):
            loads.append(
                pltpu.make_async_copy(
                    from_any.at[:, at], to_ref.at[:, at], sems.at[2 + 2 * chunk + step]
                )
            )
    for load in loads:
        load.start()
    loads[0].wait()
    loads[1].wait()
    dqn = cols_dot(dq_ref[...], weights_ref[0, :, :HALF])

    def saves(chunk):
        copies = []
        for block in range(chunk * (size // 64), (chunk + 1) * (size // 64)):
            slab = block if block < 16 else 31 - block
            row = 0 if block < 16 else 64
            from_rows = rows_ref.at[pl.ds(64 * block, 64)]
            for to_any, wanted in (
                (kept_any, core == slab % 2),
                (given_any, core != slab % 2),
            ):
                copy = pltpu.make_async_copy(
                    from_rows, to_any.at[slab // 2, pl.ds(row, 64)], sems.at[10 + block]
                )
                copies.append((wanted, copy))
        return copies

    for chunk in range(chunks):
        at = slice(size * chunk, size * chunk + size)
        loads[2 + 2 * chunk].wait()
        loads[3 + 2 * chunk].wait()
        rows_ref[at, :] = (
            cols_dot(wide(dk_ref.at[:, at]), weights_ref[0, :, HALF:WIDTH])
            + cols_dot(wide(dv_ref.at[:, at]), weights_ref[1, :, :HALF])
        ).astype(jnp.bfloat16)
        for tile, rows in ((tile_a, slice(0, 128)), (tile_b, slice(128, 256))):

            @pl.when((tile >= chunk * size // TILE) & (tile < (chunk + 1) * size // TILE))
            def _():
                own = pl.ds(pl.multiple_of(tile * TILE, TILE), TILE)
                rows_ref[own, :] = (rows_ref[own, :].astype(jnp.float32) + dqn[rows]).astype(
                    jnp.bfloat16
                )

        for wanted, copy in saves(chunk):
            pl.when(wanted)(copy.start)
    for chunk in range(chunks):
        for wanted, copy in saves(chunk):
            pl.when(wanted)(copy.wait)


def up_kernel(place_ref, cot_ref, w_out_ref, up_ref):
    def one_block(block, carry):
        at = pl.ds(pl.multiple_of(block * 512, 512), 512)
        up_ref[at, :] = cols_dot(cot_ref[at, :], w_out_ref[...]).astype(jnp.bfloat16)
        return carry

    lax.fori_loop(0, cot_ref.shape[0] // 512, one_block, 0)


def expert_units(place_ref, rows_ref, partner_ref, up_ref, w_in_ref, side_ref, keep):
    block_rows = rows_ref.shape[0]
    lane = lax.broadcasted_iota(jnp.int32, (block_rows, 128), 1)
    rows = rows_ref[...]
    logits = plain_dot(rows, side_ref[...])
    partner = partner_ref[...].astype(jnp.float32)
    own = jnp.sum(jnp.where(lane == place_ref[2], logits, 0.0), axis=-1, keepdims=True)
    also = jnp.sum(
        jnp.where(lane.astype(jnp.float32) == partner, logits, 0.0), axis=-1, keepdims=True
    )
    top = jnp.maximum(own, also)
    own, also = jnp.exp(own - top), jnp.exp(also - top)
    gate = own / (own + also)
    for step in range(w_in_ref.shape[1] // 256):
        lanes = slice(256 * step, 256 * step + 256)
        value, slope = gelu_parts(plain_dot(rows, w_in_ref[:, lanes]))
        keep(lanes, value, gate, gate * up_ref[:, lanes].astype(jnp.float32) * slope)


def expert_kernel(
    place_ref,
    rows_ref,
    partner_ref,
    up_ref,
    w_in_ref,
    w_out_ref,
    side_ref,
    back_ref,
    inner,
    d_pre,
):
    def keep(lanes, value, gate, d_value):
        inner[:, lanes] = value.astype(jnp.bfloat16)
        d_pre[:, lanes] = d_value.astype(jnp.bfloat16)

    expert_units(place_ref, rows_ref, partner_ref, up_ref, w_in_ref, side_ref, keep)
    back_ref[:, :WIDTH] = plain_dot(inner[...], w_out_ref[...]).astype(jnp.bfloat16)
    back_ref[:, WIDTH:] = cols_dot(d_pre[...], w_in_ref[...]).astype(jnp.bfloat16)


def again_kernel(
    place_ref, rows_ref, partner_ref, up_ref, w_in_ref, side_ref, gated_ref, d_pre_ref
):
    def keep(lanes, value, gate, d_value):
        gated_ref[:, lanes] = (gate * value).astype(jnp.bfloat16)
        d_pre_ref[:, lanes] = d_value.astype(jnp.bfloat16)

    expert_units(place_ref, rows_ref, partner_ref, up_ref, w_in_ref, side_ref, keep)


def call(kernel, shapes, scratch, flops, place, *operands, anywhere=(), saved=0):
    outs = tuple(jax.ShapeDtypeStruct(shape, dtype) for shape, dtype in shapes)
    in_vmem, left = pl.BlockSpec(memory_space=pltpu.VMEM), pl.BlockSpec(memory_space=pl.ANY)
    specs = [left if at in anywhere else in_vmem for at in range(len(operands))]
    if place is not None:
        specs, operands = [pl.BlockSpec(memory_space=pltpu.SMEM)] + specs, (place, *operands)
    scratch = [pltpu.VMEM(shape, dtype) for shape, dtype in scratch]
    if anywhere:
        scratch.append(pltpu.SemaphoreType.DMA((48,)))
    return pl.pallas_call(
        kernel,
        out_shape=outs,
        in_specs=specs,
        out_specs=tuple(left if at < saved else in_vmem for at in range(len(outs))),
        scratch_shapes=scratch,
        compiler_params=pltpu.CompilerParams(vmem_limit_bytes=60 * 2**20),
        cost_estimate=pl.CostEstimate(
            flops=flops, bytes_accessed=16 * 2**20, transcendentals=3 * 10**6
        ),
    )(*operands)


ROWS = 16 * TILE


def near_biases(table):
    shapes = (((PAIRS, 2 * TILE, 2 * TILE), jnp.float32),)
    return call(near_kernel, shapes, (), 10**7, table)[0]


def attend(*operands):
    low, full = jnp.bfloat16, jnp.float32
    shapes = (
        ((ROWS, WIDTH), low),
        ((PAIRS, ROWS, 128), low),
        ((PAIRS, ROWS, 128), low),
        ((2 * TILE, HALF), low),
        ((2, TILE, HALF), low),
        ((4 * TILE, 128), full),
        ((WIDTH, 128), low),
    )
    scratch = (
        ((4 * TILE, ROWS), full),
        ((9, CHUNK, CHUNK), full),
        ((4 * TILE, 128), low),
        ((ROWS, WIDTH), low),
        ((2, WIDTH, SIDE_END), low),
        ((PAIRS, 2 * TILE, 2 * TILE), full),
        *shapes[:3],
    )
    return call(
        attend_kernel, shapes, scratch, 8 * 10**9, *operands, anywhere=(0, 1, 2, 3), saved=3
    )


def attend_back(*operands):
    low, full = jnp.bfloat16, jnp.float32
    shapes = (
        ((PAIRS, ROWS, 128), low),
        ((PAIRS, ROWS, 128), low),
        ((2, WIDTH, SIDE_END), low),
        ((2 * TILE, HALF), low),
    )
    scratch = (
        ((4 * TILE, ROWS), full),
        ((9, CHUNK, CHUNK), full),
        ((48, TILE), full),
        ((2, TILE, WIDTH), low),
        ((2 * TILE, HALF), low),
        ((4 * TILE, 128), low),
        ((4 * TILE, 128), low),
        ((4 * TILE, 1), full),
        ((4 * TILE, 1), full),
        ((128, 4 * TILE), low),
        ((128, 4 * TILE), low),
        ((128, ROWS), full),
        ((128, ROWS), full),
        ((PAIRS, ROWS, 128), low),
        ((PAIRS, ROWS, 128), low),
        ((PAIRS, 2 * TILE, 2 * TILE), full),
        ((WIDTH, ROWS), low),
        ((WIDTH, 2 * TILE), low),
        *shapes[:3],
    )
    return call(
        back_kernel, shapes, scratch, 12 * 10**9, *operands, anywhere=(1, 2, 7, 8, 9), saved=3
    )


def mid(rows, *operands):
    low, full = jnp.bfloat16, jnp.float32
    shapes = (((TILE, WIDTH), full), ((TILE, WIDTH), low), ((rows, WIDTH), low))
    return call(mid_kernel, shapes, (), 10**9, *operands)


def token_side(*operands):
    low, full = jnp.bfloat16, jnp.float32
    shapes = (
        ((TILE, WIDTH), low),
        ((TILE, WIDTH), full),
        ((TILE, WIDTH), low),
        ((WIDTH, 128), low),
    )
    return call(token_kernel, shapes, (), 10**9, None, *operands)


def up_pass(rows, hidden_units, *operands):
    (up,) = call(up_kernel, (((rows, hidden_units), jnp.bfloat16),), (), 3 * 10**9, *operands)
    return up


def spread(*operands):
    low = jnp.bfloat16
    shapes = (((8, TILE, WIDTH), low),) * 2
    scratch = (
        ((PAIRS, ROWS, 128), low),
        ((PAIRS, ROWS, 128), low),
        ((2, WIDTH, SIDE_END), low),
        ((ROWS, WIDTH), low),
    )
    return call(
        spread_kernel, shapes, scratch, 3 * 10**9, *operands, anywhere=(1, 2, 3), saved=2
    )


def by_rows(kernel, outs, scratch, flops, place, blocked, whole):
    count, block = blocked[0].shape[0], EXPERT_BLOCK
    low = jnp.bfloat16

    def spec(columns):
        return pl.BlockSpec((block, columns), lambda i: (i, 0))

    return pl.pallas_call(
        kernel,
        grid=(count // block,),
        out_shape=tuple(jax.ShapeDtypeStruct((count, columns), low) for columns in outs),
        in_specs=[
            pl.BlockSpec(memory_space=pltpu.SMEM),
            *(spec(array.shape[1]) for array in blocked),
            *(pl.BlockSpec(memory_space=pltpu.VMEM) for _ in whole),
        ],
        out_specs=tuple(spec(columns) for columns in outs),
        scratch_shapes=[pltpu.VMEM((block, columns), low) for columns in scratch],
        compiler_params=pltpu.CompilerParams(vmem_limit_bytes=EXPERT_VMEM),
        cost_estimate=pl.CostEstimate(
            flops=flops, bytes_accessed=20 * 2**20, transcendentals=2 * 10**6
        ),
    )(place, *blocked, *whole)


def expert_pass(place, rows, partner, up, w_in, w_out, side):
    units = w_in.shape[1]
    (back,) = by_rows(
        expert_kernel,
        (2 * WIDTH,),
        (units, units),
        8 * 10**9,
        place,
        (rows, partner, up),
        (w_in, w_out, side),
    )
    return back


def expert_again(place, rows, partner, up, w_in, side):
    units = w_in.shape[1]
    return by_rows(
        again_kernel, (units, units), (), 3 * 10**9, place, (rows, partner, up), (w_in, side)
    )


def swap(shard):
    return lax.ppermute(shard, CORE, [(0, 1), (1, 0)])


def to_all(shard, axes):
    devices = lax.axis_size(axes)
    return lax.all_to_all(
        jnp.broadcast_to(shard[None], (devices, *shard.shape)), axes, 0, 0, tiled=True
    )


def quad_exchange(blocks):
    me = lax.axis_index(QUAD)
    got = [lax.dynamic_index_in_dim(blocks, me, 0, keepdims=False)]
    for step in range(1, 4):
        part = lax.dynamic_index_in_dim(blocks, me ^ step, 0, keepdims=False)
        got.append(lax.ppermute(part, QUAD, [(i, i ^ step) for i in range(4)]))
    rows = []
    for place in range(4):
        row = got[0]
        for step in range(1, 4):
            row = jnp.where(me ^ step == place, got[step], row)
        rows.append(row)
    return jnp.stack(rows)


def exchange(blocks, axes):
    return lax.all_to_all(blocks, axes, split_axis=0, concat_axis=0, tiled=True)


def gelu_parts(pre):
    root = math.sqrt(2.0 / math.pi)
    square = pre * pre
    curve = jnp.tanh(pre * (root + (root * 0.044715) * square))
    share = 0.5 + 0.5 * curve
    value = pre * share
    slope = share + value * (1.0 - share) * (2 * root + (6 * root * 0.044715) * square)
    return value, slope


def shards(
    tokens,
    cotangent,
    routes,
    w_query,
    w_key,
    w_value,
    w_output,
    w_router,
    gain_attn,
    gain_ffn,
    bias_table,
    w_in,
    w_out,
):
    f32, bf16 = jnp.float32, jnp.bfloat16
    core = lax.axis_index(CORE)
    chip = lax.axis_index(CHIPS)
    expert = lax.axis_index(SEQ_CTX)
    on_first = core == 0
    tok_count, model_width = tokens.shape[1:]
    local_rows = w_query.shape[0]
    expert_count = w_router.shape[1]
    place = jnp.stack([chip, core, expert]).astype(jnp.int32)

    own_tokens = tokens[0]
    mine = to_all(own_tokens, CHIPS)
    other = swap(mine)

    quarters = jnp.stack([jnp.stack([w_query, w_key]), jnp.stack([w_value, w_output])])
    quarters = quarters.reshape(2, 2, local_rows, 2, HALF).transpose(3, 0, 2, 1, 4)
    quarters = quarters.reshape(2, 2, local_rows, 2 * HALF)
    extra = jnp.concatenate(
        [
            w_router,
            gain_attn[:, None],
            gain_ffn[:, None],
            jnp.zeros((local_rows, 128 - expert_count - 2), bf16),
        ],
        axis=1,
    )
    own_routes = routes.reshape(-1, 128).astype(bf16)
    own_routes = jnp.pad(own_routes, ((0, local_rows - own_routes.shape[0]), (0, 0)))
    extra = jnp.stack([extra, own_routes])
    extra = jnp.broadcast_to(extra[None], (2, *extra.shape))
    packed_weights = jnp.concatenate([quarters, extra], axis=-1).reshape(4, local_rows, -1)
    group_rows = 4 * local_rows
    weight_rows = quad_exchange(packed_weights).reshape(group_rows, -1)
    all_weights = to_all(weight_rows, SAME_CORE).reshape(2, model_width, -1)
    own_table = lax.dynamic_slice_in_dim(bias_table, core * (HEADS // 2), HEADS // 2, 1)
    near = near_biases(own_table)

    route_ids = routes[0]
    capacity = max(2, 2 * TOP * tok_count // expert_count)
    flat_ids = route_ids.reshape(-1)
    flat_marks = (flat_ids[:, None] == jnp.arange(expert_count, dtype=jnp.int32)).astype(jnp.int32)
    earlier = jnp.cumsum(flat_marks, axis=0, dtype=jnp.int32) - flat_marks
    slot_ids = jnp.sum(earlier * flat_marks, axis=-1, dtype=jnp.int32)
    row_index = (flat_ids * capacity + slot_ids).reshape(tok_count, TOP)
    exp_count = lax.axis_size("exp")
    device_count = expert_count * exp_count
    slots = jnp.arange(device_count * capacity, dtype=jnp.int32)
    slots = slots // (exp_count * capacity) * capacity + slots % capacity
    pick = (row_index.T[:, :, None] == slots[None, None, :]).astype(bf16)
    pack = (row_index.T[:, None, :] == slots[None, :, None]).astype(bf16)

    def to_experts(rows):
        return exchange(rows.reshape(device_count, capacity, -1), SEQ_CTX_EXP)

    cot_own = cotangent[0]
    all_pack = pack[0] + pack[1]
    cot_rows = plain_dot(all_pack, cot_own).astype(bf16)
    near, cot_rows, other, all_weights = lax.optimization_barrier(
        (near, cot_rows, other, all_weights)
    )
    cot_there = to_experts(cot_rows)
    wo_half = all_weights[1, :, HALF:model_width]
    wo_other = swap(wo_half)

    normed_all, keys, values, queries, attended, log_totals, side = attend(
        place, mine, other, all_weights, near
    )

    attended_other = swap(attended)
    pair_attended = jnp.concatenate(
        [
            jnp.where(on_first, attended, attended_other),
            jnp.where(on_first, attended_other, attended),
        ],
        axis=-1,
    )
    hidden, normed_ffn, packed = mid(
        device_count * capacity,
        place,
        attended,
        attended_other,
        own_tokens,
        side,
        wo_half,
        wo_other,
        all_pack,
    )
    there = to_experts(packed)

    inner_in, inner_out = w_in[0], w_out[0]
    flat_rows = there.reshape(-1, model_width)
    flat_cot = cot_there.reshape(flat_rows.shape[0], -1)
    all_routes = all_weights[1, :, model_width:].reshape(device_count, local_rows, 128)
    all_routes = all_routes[:, : TOP * tok_count // 128].reshape(device_count, -1)
    all_routes = all_routes.astype(jnp.int32)
    here = all_routes == expert
    rank = jnp.cumsum(here.astype(jnp.int32), axis=1, dtype=jnp.int32) - 1
    partners = jnp.flip(all_routes.reshape(device_count, -1, TOP), axis=2)
    partners = partners.reshape(device_count, 1, -1)
    in_slot = here[:, None, :] & (
        rank[:, None, :] == jnp.arange(capacity, dtype=jnp.int32)[None, :, None]
    )
    partner = jnp.sum(jnp.where(in_slot, partners, 0), axis=2, dtype=jnp.int32)
    partner = jnp.broadcast_to(partner.reshape(-1, 1), (device_count * capacity, 128)).astype(bf16)

    flat_cot, partner = lax.optimization_barrier((flat_cot, partner))
    up = up_pass(flat_rows.shape[0], inner_in.shape[1], place, flat_cot, inner_out)
    sent_back = expert_pass(place, flat_rows, partner, up, inner_in, inner_out, side)
    returned = exchange(sent_back.reshape(device_count, capacity, -1), SEQ_CTX_EXP)
    gated, d_pre = expert_again(place, flat_rows, partner, up, inner_in, side)
    grad_out_local = rows_dot(gated, flat_cot)
    grad_in_local = rows_dot(flat_rows, d_pre)
    normed_t = normed_all.T
    att_t = pair_attended.reshape(2 * tok_count, model_width).T

    returned, grad_out_local, grad_in_local, normed_t, att_t = lax.optimization_barrier(
        (returned, grad_out_local, grad_in_local, normed_t, att_t)
    )
    output, d_hidden, d_mixed, sums_side = token_side(
        returned.reshape(device_count * capacity, -1),
        pick.reshape(TOP * tok_count, -1),
        hidden,
        normed_ffn,
        cot_own,
        route_ids,
        side,
    )
    d_mixed_other = swap(d_mixed)

    d_keys, d_values, to_sum, d_queries = attend_back(
        place,
        queries,
        keys,
        values,
        attended,
        d_mixed,
        d_mixed_other,
        log_totals,
        near,
        normed_t,
        att_t,
        sums_side,
        wo_half,
        wo_other,
    )
    groups = model_width // group_rows
    to_add = exchange(to_sum.reshape(2 * groups, group_rows, -1), SAME_CORE)
    kept, given = spread(place, d_queries, d_keys, d_values, all_weights)
    chip_sums = (kept.astype(f32) + swap(given).astype(f32)).astype(bf16)
    to_add, chip_sums = lax.optimization_barrier((to_add, chip_sums))
    d_normed = jnp.sum(exchange(chip_sums, CHIPS).astype(f32), axis=0)
    summed = jnp.sum(to_add.astype(f32), axis=0)
    source = own_tokens.astype(f32)
    inv_first = lax.rsqrt(jnp.mean(source * source, axis=-1, keepdims=True) + epsilon)
    scaled_first = side[:, expert_count].astype(f32)[None, :] * d_normed
    grad_tokens = (
        d_hidden
        + inv_first * scaled_first
        - source * inv_first**3 * jnp.mean(scaled_first * source, axis=-1, keepdims=True)
    )

    cells = jnp.broadcast_to(
        summed[None, :, model_width:].reshape(1, 1, -1), (4, 1, 128 * group_rows)
    )
    cells = jnp.pad(cells, ((0, 0), (0, 0), (0, -cells.shape[2] % summed.shape[1])))
    finals = quad_exchange(
        jnp.concatenate(
            [summed.reshape(4, local_rows, -1), cells.reshape(4, -1, summed.shape[1])], axis=1
        )
    )
    finals = finals.reshape(2, 2, -1, summed.shape[1])
    body = finals[:, :, :local_rows]

    def both(part, begin):
        return jnp.concatenate(
            [body[0, part, :, begin : begin + HALF], body[1, part, :, begin : begin + HALF]], axis=1
        )

    grad_query, grad_key, grad_value, grad_output = both(0, 0), both(0, HALF), both(1, 0), both(1, HALF)
    grad_gain_attn = (
        jnp.sum(
            grad_query * w_query.astype(f32)
            + grad_key * w_key.astype(f32)
            + grad_value * w_value.astype(f32),
            axis=1,
        )
        / gain_attn.astype(f32)
    )
    last = body[0, 0, :, model_width:] + body[1, 0, :, model_width:]
    profile = finals[:, 1, local_rows:].reshape(2, -1)[:, : 128 * group_rows]
    profile = profile.reshape(HEADS, 2, 2 * TILE).sum(axis=1)
    far = (TILE - np.arange(2 * TILE)) % (2 * TILE)
    bucket = sum((far >= border).astype(np.int32) for border in limits())
    marks = (bucket[:, None] == np.arange(BUCKETS)).astype(np.float32)
    grad_table = lax.dot_general(
        jnp.asarray(marks), profile, (((0,), (1,)), ((), ())), precision=precise
    )
    return (
        output[None],
        grad_tokens[None],
        grad_query,
        grad_key,
        grad_value,
        grad_output,
        last[:, :expert_count],
        grad_gain_attn,
        last[:, expert_count],
        grad_table,
        grad_in_local[None],
        grad_out_local[None],
    )


def solution(mesh):
    split = Mesh(
        mesh.devices.reshape(mesh.shape["seq"], 2, 4, 2, mesh.shape["exp"]),
        ("seq", "ctx_0", "ctx_1", "ctx_2", "exp"),
    )
    in_specs = (
        P(("seq", "exp"), CTX, None),
        P(("seq", "exp"), CTX, None),
        P(("seq", "exp"), CTX, None),
        P(SEQ_CTX_EXP, None),
        P(SEQ_CTX_EXP, None),
        P(SEQ_CTX_EXP, None),
        P(SEQ_CTX_EXP, None),
        P(SEQ_CTX_EXP, None),
        P(SEQ_CTX_EXP),
        P(SEQ_CTX_EXP),
        P(),
        P(SEQ_CTX, None, "exp"),
        P(SEQ_CTX, "exp", None),
    )
    out_specs = (
        P(("seq", "exp"), CTX, None),
        P(("seq", "exp"), CTX, None),
        P(SEQ_CTX_EXP, None),
        P(SEQ_CTX_EXP, None),
        P(SEQ_CTX_EXP, None),
        P(SEQ_CTX_EXP, None),
        P(SEQ_CTX_EXP, None),
        P(SEQ_CTX_EXP),
        P(SEQ_CTX_EXP),
        P(),
        P(SEQ_CTX, None, "exp"),
        P(SEQ_CTX, "exp", None),
    )
    return jax.shard_map(
        shards, mesh=split, in_specs=in_specs, out_specs=out_specs, check_vma=False
    )
```

profile of v0, /device:TPU:2, one launch (start us, length us, event | category | flops | bytes accessed | tf_op | source)
XLA Modules:
  0.0 304.8 jit_solution(8957964831965246861)
XLA Ops:
  0.7 2.2 broadcast_in_dim.77
  3.0 7.9 %all-to-all-start = ((bf16[8,128,768]{2,1,0:T(8,128)(2,1)}), bf16[8,128,768]{2,1,0:T(8,128)(2,1)S(1)}, u32[]{:S(2)}, u32[]{:S(2)}) async-start(bf16[8,128,768]{2,1,0:T(8,128)(2,1)} %broadcast_in_dim.77), calls=%async_computation | async-start | bytes 3145728 | tf_op jit(solution)/shard_map/all_to_all | solution.py:952
  14.2 14.2 %collective-permute-done.1 = bf16[6,896]{1,0:T(8,128)(2,1)S(1)} collective-permute-done((bf16[6,896]{1,0:T(8,128)(2,1)S(1)}, bf16[6,896]{1,0:T(8,128)(2,1)S(1)}, u32[]{:S(2)}, u32[]{:S(2)}) %collective-permute-start.1) | collective-permute-done | bytes 10784 | tf_op jit(solution)/shard_map/ppermute | solution.py:962
  29.8 2.2 all-to-all-done.mine_any
  32.0 1.9 broadcast_in_dim.83
  34.0 9.0 %all-to-all-start.1 = ((bf16[64,24,896]{2,1,0:T(8,128)(2,1)}), bf16[64,24,896]{2,1,0:T(8,128)(2,1)S(1)}, u32[]{:S(2)}, u32[]{:S(2)}) async-start(bf16[64,24,896]{2,1,0:T(8,128)(2,1)} %broadcast_in_dim.83), calls=%async_computation.1 | async-start | bytes 5505024 | tf_op jit(solution)/shard_map/all_to_all | solution.py:952
  45.1 2.9 shard_map.229.near_any
  50.0 28.0 %all-to-all-done.1 = bf16[64,24,896]{2,1,0:T(8,128)(2,1)S(1)} async-done(((bf16[64,24,896]{2,1,0:T(8,128)(2,1)}), bf16[64,24,896]{2,1,0:T(8,128)(2,1)S(1)}, u32[]{:S(2)}, u32[]{:S(2)}) %all-to-all-start.1) | async-done | bytes 2752544 | tf_op jit(solution)/shard_map/all_to_all | solution.py:952
  78.0 8.6 %all-to-all-start.3 = ((bf16[128,8,768]{2,1,0:T(8,128)(2,1)}), bf16[128,8,768]{2,1,0:T(8,128)(2,1)}, u32[]{:S(2)}, u32[]{:S(2)}) async-start(bf16[128,8,768]{2,1,0:T(8,128)(2,1)} %bitcast.23), calls=%async_computation.3 | async-start | bytes 3145728 | tf_op jit(solution)/shard_map/all_to_all | solution.py:973
  88.4 13.7 %shard_map.230 = (bf16[2048,768]{1,0:T(8,128)(2,1)}, bf16[3,2048,128]{2,1,0:T(8,128)(2,1)}, bf16[3,2048,128]{2,1,0:T(8,128)(2,1)}, bf16[256,384]{1,0:T(8,128)(2,...) custom-call(s32[3]{0:T(128)} %pad_add_fusion.place_ref, ...), custom_call_target="tpu_custom_call" | custom-call | flops 8000000000 | bytes 16777216 | tf_op jit(solution)/shard_map/pallas_call | solution.py:784
  104.5 3.9 %shard_map.231 = (f32[128,768]{1,0:T(8,128)}, bf16[128,768]{1,0:T(8,128)(2,1)}, bf16[1024,768]{1,0:T(8,128)(2,1)}) custom-call(s32[3]{0:T(128)} %pad_add_fusion.place_ref, bf16[2,128,384]{2,1,0:T(8,128)(2,1)} %get-tuple-element.50.mine_ref.att_ref, bf16[2,128,384]{2,1,0:T(8,128)(2,1)} %copy-done.14, bf16[128,768]{1,0:T(8,128)(2,1)} %bitcast.189, ...), custom_call_target="tpu_custom_call" | custom-call | flops 1000000000 | bytes 16777216 | tf_op jit(solution)/shard_map/pallas_call | solution.py:784
  109.6 8.9 %all-to-all-start.2 = ((bf16[128,8,768]{2,1,0:T(8,128)(2,1)}), bf16[128,8,768]{2,1,0:T(8,128)(2,1)S(1)}, u32[]{:S(2)}, u32[]{:S(2)}) async-start(bf16[128,8,768]{2,1,0:T(8,128)(2,1)} %bitcast.190), calls=%async_computation.2 | async-start | bytes 3145728 | tf_op jit(solution)/shard_map/all_to_all | solution.py:973
  119.9 2.2 select_reduce_fusion
  123.2 6.7 %shard_map.232.up_ref = bf16[1024,1536]{1,0:T(8,128)(2,1)} custom-call(s32[3]{0:T(128)} %pad_add_fusion.place_ref, bf16[1024,768]{1,0:T(8,128)(2,1)} %bitcast.24.cot_ref, bf16[1536,768]{1,0:T(8,128)(2,1)} %bitcast.211), custom_call_target="tpu_custom_call" | custom-call | flops 3000000000 | bytes 16777216 | tf_op jit(solution)/shard_map/pallas_call | solution.py:784
  129.9 12.0 %all-to-all-done.2 = bf16[128,8,768]{2,1,0:T(8,128)(2,1)S(1)} async-done(((bf16[128,8,768]{2,1,0:T(8,128)(2,1)}), bf16[128,8,768]{2,1,0:T(8,128)(2,1)S(1)}, u32[]{:S(2)}, u32[]{:S(2)}) %all-to-all-start.2) | async-done | bytes 1572896 | tf_op jit(solution)/shard_map/all_to_all | solution.py:973
  143.0 13.2 %shard_map.233 = bf16[1024,1536]{1,0:T(8,128)(2,1)} custom-call(s32[3]{0:T(128)} %pad_add_fusion.place_ref, bf16[1024,768]{1,0:T(8,128)(2,1)} %bitcast.178, bf16[1024,128]{1,0:T(8,128)(2,1)} %broadcast_in_dim.87.partner_ref, bf16[1024,1536]{1,0:T(8,128)(2,1)} %shard_map.232.up_ref, bf16[768,1536]{1,0:T(8,128)(2,1)} %bitcast.213, ...), custom_call_target="tpu_custom_call" | custom-call | flops 8000000000 | bytes 20971520 | tf_op jit(solution)/shard_map/pallas_call | solution.py:907
  156.2 7.6 %all-to-all-start.4 = ((bf16[128,8,1536]{2,1,0:T(8,128)(2,1)}), bf16[128,8,1536]{2,1,0:T(8,128)(2,1)}, u32[]{:S(2)}, u32[]{:S(2)}) async-start(bf16[128,8,1536]{2,1,0:T(8,128)(2,1)} %bitcast.186), calls=%async_computation.4 | async-start | bytes 6291456 | tf_op jit(solution)/shard_map/all_to_all | solution.py:973
  164.8 2.9 copy.125
  168.8 9.7 %shard_map.234 = (bf16[1024,1536]{1,0:T(8,128)(2,1)}, bf16[1024,1536]{1,0:T(8,128)(2,1)}) custom-call(s32[3]{0:T(128)} %pad_add_fusion.place_ref, bf16[1024,768]{1,0:T(8,128)(2,1)} %bitcast.179, bf16[1024,128]{1,0:T(8,128)(2,1)} %broadcast_in_dim.87.partner_ref, bf16[1024,1536]{1,0:T(8,128)(2,1)} %shard_map.232.up_ref, bf16[768,1536]{1,0:T(8,128)(2,1)} %bitcast.214, ...), custom_call_target="tpu_custom_call" | custom-call | flops 3000000000 | bytes 20971520 | tf_op jit(solution)/shard_map/pallas_call | solution.py:907
  178.5 7.4 %fusion.51 = f32[1536,768]{1,0:T(8,128)} fusion(bf16[1024,1536]{1,0:T(8,128)(2,1)} %get-tuple-element.56, bf16[1024,768]{1,0:T(8,128)(2,1)} %bitcast.24.cot_ref), kind=kOutput, calls=%fused_computation.139 | convolution fusion | flops 2415919104 | bytes 9437184 | tf_op jit(solution)/shard_map/dot_general | solution.py:58
  185.8 4.3 %fusion.46 = f32[768,1536]{1,0:T(8,128)} fusion(bf16[1024,1536]{1,0:T(8,128)(2,1)S(1)} %copy-done.6, bf16[128,8,768]{2,1,0:T(8,128)(2,1)S(1)} %copy-done.3), kind=kOutput, calls=%fused_computation.134 | convolution fusion | flops 2415919104 | bytes 9437184 | tf_op jit(solution)/shard_map/dot_general | solution.py:58
  190.1 13.5 %all-to-all-done.4 = bf16[128,8,1536]{2,1,0:T(8,128)(2,1)} async-done(((bf16[128,8,1536]{2,1,0:T(8,128)(2,1)}), bf16[128,8,1536]{2,1,0:T(8,128)(2,1)}, u32[]{:S(2)}, u32[]{:S(2)}) %all-to-all-start.4) | async-done | bytes 3145760 | tf_op jit(solution)/shard_map/all_to_all | solution.py:973
  203.6 4.7 %shard_map.235 = (bf16[128,768]{1,0:T(8,128)(2,1)}, f32[128,768]{1,0:T(8,128)}, bf16[128,768]{1,0:T(8,128)(2,1)}, bf16[768,128]{1,0:T(8,128)(2,1)}) custom-call(bf16[1024,1536]{1,0:T(8,128)(2,1)} %bitcast.36.back_ref, bf16[256,1024]{1,0:T(8,128)(2,1)} %compare_convert_fusion.pick_ref, f32[128,768]{1,0:T(8,128)} %get-tuple-element.60.hidden_ref, ...), custom_call_target="tpu_custom_call" | custom-call | flops 1000000000 | bytes 16777216 | tf_op jit(solution)/shard_map/pallas_call | solution.py:784
  211.6 18.6 %shard_map.236 = (bf16[3,2048,128]{2,1,0:T(8,128)(2,1)}, bf16[3,2048,128]{2,1,0:T(8,128)(2,1)}, bf16[2,768,896]{2,1,0:T(8,128)(2,1)}, bf16[256,384]{1,0:T(8,128)(2,1)}) custom-call(s32[3]{0:T(128)} %pad_add_fusion.place_ref, bf16[256,384]{1,0:T(8,128)(2,1)} %get-tuple-element.64.q_ref, bf16[3,2048,128]{2,1,0:T(8,128)(2,1)} %get-tuple-element.65.k_any, ...), custom_call_target="tpu_custom_call" | custom-call | flops 12000000000 | bytes 16777216 | tf_op jit(solution)/shard_map/pallas_call | solution.py:784
  230.1 6.0 %all-to-all-start.5 = ((bf16[64,24,896]{2,1,0:T(8,128)(2,1)}), bf16[64,24,896]{2,1,0:T(8,128)(2,1)S(1)}, u32[]{:S(2)}, u32[]{:S(2)}) async-start(bf16[64,24,896]{2,1,0:T(8,128)(2,1)} %bitcast.187), calls=%async_computation.5 | async-start | bytes 5505024 | tf_op jit(solution)/shard_map/all_to_all | solution.py:973
  236.1 9.7 %shard_map.237 = (bf16[8,128,768]{2,1,0:T(8,128)(2,1)}, bf16[8,128,768]{2,1,0:T(8,128)(2,1)}) custom-call(s32[3]{0:T(128)} %pad_add_fusion.place_ref, bf16[256,384]{1,0:T(8,128)(2,1)} %get-tuple-element.73.dq_ref, bf16[3,2048,128]{2,1,0:T(8,128)(2,1)} %get-tuple-element.74.dk_any, bf16[3,2048,128]{2,1,0:T(8,128)(2,1)} %get-tuple-element.75.dv_any, ...), custom_call_target="tpu_custom_call" | custom-call | flops 3000000000 | bytes 16777216 | tf_op jit(solution)/shard_map/pallas_call | solution.py:784
  245.9 3.6 %collective-permute-done.7 = bf16[8,128,768]{2,1,0:T(8,128)(2,1)S(1)} collective-permute-done((bf16[8,128,768]{2,1,0:T(8,128)(2,1)}, bf16[8,128,768]{2,1,0:T(8,128)(2,1)S(1)}, u32[]{:S(2)}, u32[]{:S(2)}) %collective-permute-start.7) | collective-permute-done | bytes 1572896 | tf_op jit(solution)/shard_map/ppermute | solution.py:947
  249.5 2.9 add_convert_fusion
  252.4 23.3 %all-to-all-done.5 = bf16[64,24,896]{2,1,0:T(8,128)(2,1)S(1)} async-done(((bf16[64,24,896]{2,1,0:T(8,128)(2,1)}), bf16[64,24,896]{2,1,0:T(8,128)(2,1)S(1)}, u32[]{:S(2)}, u32[]{:S(2)}) %all-to-all-start.5) | async-done | bytes 2752544 | tf_op jit(solution)/shard_map/all_to_all | solution.py:973
  276.5 2.0 collective-permute-start.10
  278.7 3.6 %all-to-all-start.6 = ((bf16[8,128,768]{2,1,0:T(8,128)(2,1)}), bf16[8,128,768]{2,1,0:T(8,128)(2,1)S(1)}, u32[]{:S(2)}, u32[]{:S(2)}) async-start(bf16[8,128,768]{2,1,0:T(8,128)(2,1)} %add_convert_fusion), calls=%async_computation.6 | async-start | bytes 3145728 | tf_op jit(solution)/shard_map/all_to_all | solution.py:973
  286.0 17.2 %all-to-all-done.6 = bf16[8,128,768]{2,1,0:T(8,128)(2,1)S(1)} async-done(((bf16[8,128,768]{2,1,0:T(8,128)(2,1)}), bf16[8,128,768]{2,1,0:T(8,128)(2,1)S(1)}, u32[]{:S(2)}, u32[]{:S(2)}) %all-to-all-start.6) | async-done | bytes 1572896 | tf_op jit(solution)/shard_map/all_to_all | solution.py:973
  (177 shorter events, 28.7 us)
Async XLA Ops:
  0.6 42.4 %copy-start = (f32[32,12]{0,1:T(8,128)S(1)}, f32[32,12]{0,1:T(8,128)}, u32[]{:S(2)}) copy-start(f32[32,12]{0,1:T(8,128)} %param.24) | copy-start | bytes 4612
  0.7 10.5 %copy-start.18 = (bf16[6,768]{1,0:T(8,128)(2,1)S(1)}, bf16[6,768]{1,0:T(8,128)(2,1)}, u32[]{:S(2)}) copy-start(bf16[6,768]{1,0:T(8,128)(2,1)} %param.19) | copy-start | bytes 27652
  0.7 10.5 %copy-start.20 = (bf16[6,768]{1,0:T(8,128)(2,1)S(1)}, bf16[6,768]{1,0:T(8,128)(2,1)}, u32[]{:S(2)}) copy-start(bf16[6,768]{1,0:T(8,128)(2,1)} %param.18) | copy-start | bytes 27652
  0.7 10.6 %copy-start.22 = (bf16[6,768]{1,0:T(8,128)(2,1)S(1)}, bf16[6,768]{1,0:T(8,128)(2,1)}, u32[]{:S(2)}) copy-start(bf16[6,768]{1,0:T(8,128)(2,1)} %param.17) | copy-start | bytes 27652
  0.7 10.7 %copy-start.28 = (bf16[6]{0:T(256)(128)(2,1)S(1)}, bf16[6]{0:T(256)(128)(2,1)}, u32[]{:S(2)}) copy-start(bf16[6]{0:T(256)(128)(2,1)} %param.23) | copy-start | bytes 40
  0.7 10.8 %copy-start.29 = (bf16[6]{0:T(256)(128)(2,1)S(1)}, bf16[6]{0:T(256)(128)(2,1)}, u32[]{:S(2)}) copy-start(bf16[6]{0:T(256)(128)(2,1)} %param.22) | copy-start | bytes 40
  0.7 11.0 %copy-start.26 = (bf16[6,64]{1,0:T(8,128)(2,1)S(1)}, bf16[6,64]{1,0:T(8,128)(2,1)}, u32[]{:S(2)}) copy-start(bf16[6,64]{1,0:T(8,128)(2,1)} %param.21) | copy-start | bytes 2308
  3.0 29.0 %all-to-all-start = ((bf16[8,128,768]{2,1,0:T(8,128)(2,1)}), bf16[8,128,768]{2,1,0:T(8,128)(2,1)S(1)}, u32[]{:S(2)}, u32[]{:S(2)}) async-start(bf16[8,128,768]{2,1,0:T(8,128)(2,1)} %broadcast_in_dim.77), calls=%async_computation | async-start | bytes 3145728 | tf_op jit(solution)/shard_map/all_to_all | solution.py:952
  11.0 34.0 %copy-start.9 = (s32[1,128,2]{2,1,0:T(8,128)}, s32[1,128,2]{2,1,0:T(8,128)S(1)}, u32[]{:S(2)}) copy-start(s32[1,128,2]{2,1,0:T(8,128)S(1)} %copy.105) | copy-start | bytes 3076
  12.0 16.4 %collective-permute-start.1 = (bf16[6,896]{1,0:T(8,128)(2,1)S(1)}, bf16[6,896]{1,0:T(8,128)(2,1)S(1)}, u32[]{:S(2)}, u32[]{:S(2)}) collective-permute-start(bf16[6,896]{1,0:T(8,128)(2,1)S(1)} %bitcast.205), channel_id=1, source_target_pairs={{0,3},{1,2},{2,1},{3,0},{4,7},{5,6},{6,5},{7,4},{8,11},{9,10},{10,... | collective-permute-start | bytes 32264 | tf_op jit(solution)/shard_map/ppermute | solution.py:962
  12.1 16.3 %collective-permute-start.2 = (bf16[6,896]{1,0:T(8,128)(2,1)S(1)}, bf16[6,896]{1,0:T(8,128)(2,1)S(1)}, u32[]{:S(2)}, u32[]{:S(2)}) collective-permute-start(bf16[6,896]{1,0:T(8,128)(2,1)S(1)} %bitcast.206), channel_id=1, source_target_pairs={{0,2},{1,3},{2,0},{3,1},{4,6},{5,7},{6,4},{7,5},{8,10},{9,11},{10,... | collective-permute-start | bytes 32264 | tf_op jit(solution)/shard_map/ppermute | solution.py:962
  12.9 16.8 %collective-permute-start.3 = (bf16[6,896]{1,0:T(8,128)(2,1)S(1)}, bf16[6,896]{1,0:T(8,128)(2,1)S(1)}, u32[]{:S(2)}, u32[]{:S(2)}) collective-permute-start(bf16[6,896]{1,0:T(8,128)(2,1)S(1)} %bitcast.207), channel_id=1, source_target_pairs={{0,1},{1,0},{2,3},{3,2},{4,5},{5,4},{6,7},{7,6},{8,9},{9,8},{10,11... | collective-permute-start | bytes 32264 | tf_op jit(solution)/shard_map/ppermute | solution.py:962
  34.0 44.0 %all-to-all-start.1 = ((bf16[64,24,896]{2,1,0:T(8,128)(2,1)}), bf16[64,24,896]{2,1,0:T(8,128)(2,1)S(1)}, u32[]{:S(2)}, u32[]{:S(2)}) async-start(bf16[64,24,896]{2,1,0:T(8,128)(2,1)} %broadcast_in_dim.83), calls=%async_computation.1 | async-start | bytes 5505024 | tf_op jit(solution)/shard_map/all_to_all | solution.py:952
  43.0 35.0 %collective-permute-start = (bf16[8,128,768]{2,1,0:T(8,128)(2,1)}, bf16[8,128,768]{2,1,0:T(8,128)(2,1)}, u32[]{:S(2)}, u32[]{:S(2)}) collective-permute-start(bf16[8,128,768]{2,1,0:T(8,128)(2,1)} %copy-done.8), channel_id=1, source_target_pairs={{0,2},{2,0},{1,3},{3,1},{4,6},{6,4},{5,7},{7,5},{8,10},{10,8},{9,1... | collective-permute-start | bytes 4718600 | tf_op jit(solution)/shard_map/ppermute | solution.py:947
  48.3 39.8 %copy-start.10 = (bf16[1024,128]{1,0:T(8,128)(2,1)}, bf16[1024,128]{1,0:T(8,128)(2,1)S(1)}, u32[]{:S(2)}) copy-start(bf16[1024,128]{1,0:T(8,128)(2,1)S(1)} %fusion.6.pack_ref) | copy-start | bytes 786436
  78.0 31.6 %all-to-all-start.3 = ((bf16[128,8,768]{2,1,0:T(8,128)(2,1)}), bf16[128,8,768]{2,1,0:T(8,128)(2,1)}, u32[]{:S(2)}, u32[]{:S(2)}) async-start(bf16[128,8,768]{2,1,0:T(8,128)(2,1)} %bitcast.23), calls=%async_computation.3 | async-start | bytes 3145728 | tf_op jit(solution)/shard_map/all_to_all | solution.py:973
  88.1 15.7 %collective-permute-start.5 = (bf16[768,384]{1,0:T(8,128)(2,1)}, bf16[768,384]{1,0:T(8,128)(2,1)}, u32[]{:S(2)}, u32[]{:S(2)}) collective-permute-start(bf16[768,384]{1,0:T(8,128)(2,1)} %slice_bitcast_fusion.wo_mine_ref), channel_id=1, source_target_pairs={{0,2},{2,0},{1,3},{3,1},{4,6},{6,4},{5,7},{7,5},{8,10},{10,8},{9,1... | collective-permute-start | bytes 1769480 | tf_op jit(solution)/shard_map/ppermute | solution.py:947
  102.1 1.7 collective-permute-start.4
  109.6 32.2 %all-to-all-start.2 = ((bf16[128,8,768]{2,1,0:T(8,128)(2,1)}), bf16[128,8,768]{2,1,0:T(8,128)(2,1)S(1)}, u32[]{:S(2)}, u32[]{:S(2)}) async-start(bf16[128,8,768]{2,1,0:T(8,128)(2,1)} %bitcast.190), calls=%async_computation.2 | async-start | bytes 3145728 | tf_op jit(solution)/shard_map/all_to_all | solution.py:973
  156.2 47.4 %all-to-all-start.4 = ((bf16[128,8,1536]{2,1,0:T(8,128)(2,1)}), bf16[128,8,1536]{2,1,0:T(8,128)(2,1)}, u32[]{:S(2)}, u32[]{:S(2)}) async-start(bf16[128,8,1536]{2,1,0:T(8,128)(2,1)} %bitcast.186), calls=%async_computation.4 | async-start | bytes 6291456 | tf_op jit(solution)/shard_map/all_to_all | solution.py:973
  208.3 2.6 collective-permute-start.6
  230.1 45.6 %all-to-all-start.5 = ((bf16[64,24,896]{2,1,0:T(8,128)(2,1)}), bf16[64,24,896]{2,1,0:T(8,128)(2,1)S(1)}, u32[]{:S(2)}, u32[]{:S(2)}) async-start(bf16[64,24,896]{2,1,0:T(8,128)(2,1)} %bitcast.187), calls=%async_computation.5 | async-start | bytes 5505024 | tf_op jit(solution)/shard_map/all_to_all | solution.py:973
  245.8 3.7 %collective-permute-start.7 = (bf16[8,128,768]{2,1,0:T(8,128)(2,1)}, bf16[8,128,768]{2,1,0:T(8,128)(2,1)S(1)}, u32[]{:S(2)}, u32[]{:S(2)}) collective-permute-start(bf16[8,128,768]{2,1,0:T(8,128)(2,1)} %get-tuple-element.77), channel_id=1, source_target_pairs={{0,2},{2,0},{1,3},{3,1},{4,6},{6,4},{5,7},{7,5},{8,10},{10,8},{9,1... | collective-permute-start | bytes 4718600 | tf_op jit(solution)/shard_map/ppermute | solution.py:947
  252.4 26.1 %copy-start.12 = (bf16[768,128]{1,0:T(8,128)(2,1)S(1)}, bf16[768,128]{1,0:T(8,128)(2,1)}, u32[]{:S(2)}) copy-start(bf16[768,128]{1,0:T(8,128)(2,1)} %get-tuple-element.51.side_ref) | copy-start | bytes 589828
  276.3 6.1 %collective-permute-start.8 = (f32[10,896]{1,0:T(8,128)S(1)}, f32[10,896]{1,0:T(8,128)S(1)}, u32[]{:S(2)}, u32[]{:S(2)}) collective-permute-start(f32[10,896]{1,0:T(8,128)S(1)} %get-tuple-element.104), channel_id=1, source_target_pairs={{0,3},{1,2},{2,1},{3,0},{4,7},{5,6},{6,5},{7,4},{8,11},{9,10},{10,... | collective-permute-start | bytes 107528 | tf_op jit(solution)/shard_map/ppermute | solution.py:962
  276.4 6.0 %collective-permute-start.9 = (f32[10,896]{1,0:T(8,128)S(1)}, f32[10,896]{1,0:T(8,128)S(1)}, u32[]{:S(2)}, u32[]{:S(2)}) collective-permute-start(f32[10,896]{1,0:T(8,128)S(1)} %get-tuple-element.105), channel_id=1, source_target_pairs={{0,2},{1,3},{2,0},{3,1},{4,6},{5,7},{6,4},{7,5},{8,10},{9,11},{10,... | collective-permute-start | bytes 107528 | tf_op jit(solution)/shard_map/ppermute | solution.py:962
  276.5 5.9 %collective-permute-start.10 = (f32[10,896]{1,0:T(8,128)S(1)}, f32[10,896]{1,0:T(8,128)S(1)}, u32[]{:S(2)}, u32[]{:S(2)}) collective-permute-start(f32[10,896]{1,0:T(8,128)S(1)} %get-tuple-element.103), channel_id=1, source_target_pairs={{0,1},{1,0},{2,3},{3,2},{4,5},{5,4},{6,7},{7,6},{8,9},{9,8},{10,11... | collective-permute-start | bytes 107528 | tf_op jit(solution)/shard_map/ppermute | solution.py:962
  278.7 24.5 %all-to-all-start.6 = ((bf16[8,128,768]{2,1,0:T(8,128)(2,1)}), bf16[8,128,768]{2,1,0:T(8,128)(2,1)S(1)}, u32[]{:S(2)}, u32[]{:S(2)}) async-start(bf16[8,128,768]{2,1,0:T(8,128)(2,1)} %add_convert_fusion), calls=%async_computation.6 | async-start | bytes 3145728 | tf_op jit(solution)/shard_map/all_to_all | solution.py:973
  282.3 21.1 %copy-start.7 = (bf16[1,128,768]{2,1,0:T(8,128)(2,1)S(1)}, bf16[1,128,768]{2,1,0:T(8,128)(2,1)}, u32[]{:S(2)}) copy-start(bf16[1,128,768]{2,1,0:T(8,128)(2,1)} %param.14) | copy-start | bytes 589828
  282.3 21.3 %copy-start.11 = (f32[128,768]{1,0:T(8,128)S(1)}, f32[128,768]{1,0:T(8,128)}, u32[]{:S(2)}) copy-start(f32[128,768]{1,0:T(8,128)} %get-tuple-element.63) | copy-start | bytes 1179652
  282.4 22.2 %copy-start.1 = (f32[32,12]{0,1:T(8,128)S(1)}, f32[32,12]{0,1:T(8,128)}, u32[]{:S(2)}) copy-start(f32[32,12]{0,1:T(8,128)} %param.24) | copy-start | bytes 4612
  282.6 21.9 %copy-start.24 = (f32[6,128]{1,0:T(8,128)}, f32[6,128]{1,0:T(8,128)S(1)}, u32[]{:S(2)}) copy-start(f32[6,128]{1,0:T(8,128)S(1)} %fusion.43) | copy-start | bytes 9220
  (17 other events, 100.3 us)
where the time goes:
time: 311 us; the launch traced here: 305 us
  waiting for transfers between devices  118 us (38%)
  Pallas kernels  83 us (27%)
  starting transfers between devices  58.2 us (19%)
  local copies, waits for them, and re-layouts  17.4 us (6%)
  matrix products  14.2 us (5%)
  other arithmetic  12.4 us (4%)
    all_to_all x5, waiting for transfers between devices, exchange(): return lax.all_to_all(blocks, axes, split_axis=0, concat_axis=0, tiled=True)  67.1 us
    pallas_call x7, Pallas kernels, call(): pl.pallas_call(kernel, out_shape=outs, in_specs=specs, out_specs=tuple((l...  60.1 us
    all_to_all x5, starting transfers between devices, exchange(): return lax.all_to_all(blocks, axes, split_axis=0, concat_axis=0, tiled=True)  34.7 us
    all_to_all x2, waiting for transfers between devices, to_all(): lax.all_to_all(jnp.broadcast_to(shard[None], (devices, *shard.shape)), ax...  30.2 us
    pallas_call x2, Pallas kernels, by_rows(): pl.pallas_call(kernel, grid=(count // block,), out_shape=tuple((jax.Shape...  22.9 us
    all_to_all x2, starting transfers between devices, to_all(): lax.all_to_all(jnp.broadcast_to(shard[None], (devices, *shard.shape)), ax...  16.9 us
    ppermute x6, waiting for transfers between devices, quad_exchange(): got.append(lax.ppermute(part, QUAD, [(i, i ^ step) for i in range(4)]))  15.4 us
    dot_general x2, matrix products, rows_dot(): lax.dot_general(first_op, second_op, (((0,), (0,)), ((), ())), preferred_...  11.7 us
  transfers between devices with their start and end apart: 18, of which 12 were waited for; matrix products, arithmetic and copies ran while one was open for 12% of the time, Pallas kernels for 15%

commit v1 on v0

--- a/solution.py
+++ b/solution.py
@@ -444,19 +444,19 @@
 
 def back_kernel(
     place_ref,
-    q_ref,
+    q_any,
     k_any,
     v_any,
-    att_ref,
-    mixed_ref,
-    mixed_other_ref,
-    lse_ref,
+    att_any,
+    mixed_any,
+    mixed_other_any,
+    lse_any,
     near_any,
     normed_t_any,
     att_t_any,
-    side_ref,
-    wo_mine_ref,
-    wo_other_ref,
+    side_any,
+    wo_mine_any,
+    wo_other_any,
     dk_any,
     dv_any,
     sums_any,
@@ -482,6 +482,12 @@
     dk_ref,
     dv_ref,
     sums_ref,
+    q_ref,
+    att_ref,
+    lse_ref,
+    side_ref,
+    wo_mine_ref,
+    wo_other_ref,
     sems,
 ):
     load_normed = pltpu.make_async_copy(normed_t_any, normed_t_ref, sems.at[0])
@@ -504,20 +510,41 @@
         pltpu.make_async_copy(sums_ref.at[part], sums_any.at[part], sems.at[4 + part])
         for part in range(2)
     ]
+    core = place_ref[1]
+    first = [
+        pltpu.make_async_copy(from_any, to_ref, sems.at[26 + step])
+        for step, (from_any, to_ref) in enumerate(
+            (
+                (mixed_any, d_mixed.at[core]),
+                (mixed_other_any, d_mixed.at[1 - core]),
+                (wo_mine_any, wo_mine_ref),
+                (wo_other_any, wo_other_ref),
+            )
+        )
+    ]
+    second = [
+        pltpu.make_async_copy(from_any, to_ref, sems.at[30 + step])
+        for step, (from_any, to_ref) in enumerate(
+            ((q_any, q_ref), (att_any, att_ref), (lse_any, lse_ref), (side_any, side_ref))
+        )
+    ]
+    for load in (*first, *second):
+        load.start()
     for pair in range(PAIRS):
         for load in loads_of(pair):
             load.start()
     load_normed.start()
     load_att.start()
     tile_a, tile_b = own_tiles(place_ref)
-    core = place_ref[1]
     fill_bias(bias_full, place_ref)
-    d_mixed[core] = mixed_ref[...]
-    d_mixed[1 - core] = mixed_other_ref[...]
+    for load in first:
+        load.wait()
     d_att[...] = (
         cols_dot(tile_order(d_mixed, core_rows(core)), wo_mine_ref[core_rows(core), :])
         + cols_dot(tile_order(d_mixed, core_rows(1 - core)), wo_other_ref[core_rows(core), :])
     ).astype(jnp.bfloat16)
+    for load in second:
+        load.wait()
     units = later_units(tile_a)
     reach = tile_a // 2
 
@@ -738,7 +765,8 @@
     for step in range(w_in_ref.shape[1] // 256):
         lanes = slice(256 * step, 256 * step + 256)
         value, slope = gelu_parts(plain_dot(rows, w_in_ref[:, lanes]))
-        keep(lanes, value, gate, gate * up_ref[:, lanes].astype(jnp.float32) * slope)
+        keep(lanes, value, gate, up_ref[:, lanes].astype(jnp.float32) * slope)
+    return gate
 
 
 def expert_kernel(
@@ -757,9 +785,9 @@
         inner[:, lanes] = value.astype(jnp.bfloat16)
         d_pre[:, lanes] = d_value.astype(jnp.bfloat16)
 
-    expert_units(place_ref, rows_ref, partner_ref, up_ref, w_in_ref, side_ref, keep)
+    gate = expert_units(place_ref, rows_ref, partner_ref, up_ref, w_in_ref, side_ref, keep)
     back_ref[:, :WIDTH] = plain_dot(inner[...], w_out_ref[...]).astype(jnp.bfloat16)
-    back_ref[:, WIDTH:] = cols_dot(d_pre[...], w_in_ref[...]).astype(jnp.bfloat16)
+    back_ref[:, WIDTH:] = (gate * cols_dot(d_pre[...], w_in_ref[...])).astype(jnp.bfloat16)
 
 
 def again_kernel(
@@ -767,7 +795,7 @@
 ):
     def keep(lanes, value, gate, d_value):
         gated_ref[:, lanes] = (gate * value).astype(jnp.bfloat16)
-        d_pre_ref[:, lanes] = d_value.astype(jnp.bfloat16)
+        d_pre_ref[:, lanes] = (gate * d_value).astype(jnp.bfloat16)
 
     expert_units(place_ref, rows_ref, partner_ref, up_ref, w_in_ref, side_ref, keep)
 
@@ -855,9 +883,15 @@
         ((WIDTH, ROWS), low),
         ((WIDTH, 2 * TILE), low),
         *shapes[:3],
+        shapes[3],
+        ((2, TILE, HALF), low),
+        ((4 * TILE, 128), full),
+        ((WIDTH, 128), low),
+        ((WIDTH, HALF), low),
+        ((WIDTH, HALF), low),
     )
     return call(
-        back_kernel, shapes, scratch, 12 * 10**9, *operands, anywhere=(1, 2, 7, 8, 9), saved=3
+        back_kernel, shapes, scratch, 12 * 10**9, *operands, anywhere=range(13), saved=3
     )
 
 

time: 311 us -> 310 us (level)
  no operation moved by 1% of the time
where the time goes in v1:
time: 310 us; the launch traced here: 304 us
  waiting for transfers between devices  118 us (38%)
  Pallas kernels  82.8 us (27%)
  starting transfers between devices  58.2 us (19%)
  local copies, waits for them, and re-layouts  17.4 us (6%)
  matrix products  14.2 us (5%)
  other arithmetic  12.4 us (4%)
    all_to_all x5, waiting for transfers between devices, exchange(): return lax.all_to_all(blocks, axes, split_axis=0, concat_axis=0, tiled=True)  66.9 us
    pallas_call x7, Pallas kernels, call(): pl.pallas_call(kernel, out_shape=outs, in_specs=specs, out_specs=tuple((l...  59.8 us
    all_to_all x5, starting transfers between devices, exchange(): return lax.all_to_all(blocks, axes, split_axis=0, concat_axis=0, tiled=True)  34.7 us
    all_to_all x2, waiting for transfers between devices, to_all(): lax.all_to_all(jnp.broadcast_to(shard[None], (devices, *shard.shape)), ax...  30.2 us
    pallas_call x2, Pallas kernels, by_rows(): pl.pallas_call(kernel, grid=(count // block,), out_shape=tuple((jax.Shape...  23 us
    all_to_all x2, starting transfers between devices, to_all(): lax.all_to_all(jnp.broadcast_to(shard[None], (devices, *shard.shape)), ax...  16.9 us
    ppermute x6, waiting for transfers between devices, quad_exchange(): got.append(lax.ppermute(part, QUAD, [(i, i ^ step) for i in range(4)]))  15.4 us
    dot_general x2, matrix products, rows_dot(): lax.dot_general(first_op, second_op, (((0,), (0,)), ((), ())), preferred_...  11.7 us
  transfers between devices with their start and end apart: 18, of which 12 were waited for; matrix products, arithmetic and copies ran while one was open for 12% of the time, Pallas kernels for 15%

profile of v1, /device:TPU:2, one launch (start us, length us, event | category | flops | bytes accessed | tf_op | source)
XLA Modules:
  0.0 304.3 jit_solution(3620392096834812683)
XLA Ops:
  0.7 2.2 broadcast_in_dim.77
  3.0 7.9 %all-to-all-start = ((bf16[8,128,768]{2,1,0:T(8,128)(2,1)}), bf16[8,128,768]{2,1,0:T(8,128)(2,1)S(1)}, u32[]{:S(2)}, u32[]{:S(2)}) async-start(bf16[8,128,768]{2,1,0:T(8,128)(2,1)} %broadcast_in_dim.77), calls=%async_computation | async-start | bytes 3145728 | tf_op jit(solution)/shard_map/all_to_all | solution.py:986
  14.2 14.2 %collective-permute-done.1 = bf16[6,896]{1,0:T(8,128)(2,1)S(1)} collective-permute-done((bf16[6,896]{1,0:T(8,128)(2,1)S(1)}, bf16[6,896]{1,0:T(8,128)(2,1)S(1)}, u32[]{:S(2)}, u32[]{:S(2)}) %collective-permute-start.1) | collective-permute-done | bytes 10784 | tf_op jit(solution)/shard_map/ppermute | solution.py:996
  29.8 2.2 all-to-all-done.mine_any
  32.0 1.9 broadcast_in_dim.83
  34.0 9.0 %all-to-all-start.1 = ((bf16[64,24,896]{2,1,0:T(8,128)(2,1)}), bf16[64,24,896]{2,1,0:T(8,128)(2,1)S(1)}, u32[]{:S(2)}, u32[]{:S(2)}) async-start(bf16[64,24,896]{2,1,0:T(8,128)(2,1)} %broadcast_in_dim.83), calls=%async_computation.1 | async-start | bytes 5505024 | tf_op jit(solution)/shard_map/all_to_all | solution.py:986
  45.1 2.9 shard_map.229.near_any
  50.0 28.0 %all-to-all-done.1 = bf16[64,24,896]{2,1,0:T(8,128)(2,1)S(1)} async-done(((bf16[64,24,896]{2,1,0:T(8,128)(2,1)}), bf16[64,24,896]{2,1,0:T(8,128)(2,1)S(1)}, u32[]{:S(2)}, u32[]{:S(2)}) %all-to-all-start.1) | async-done | bytes 2752544 | tf_op jit(solution)/shard_map/all_to_all | solution.py:986
  78.0 8.6 %all-to-all-start.3 = ((bf16[128,8,768]{2,1,0:T(8,128)(2,1)}), bf16[128,8,768]{2,1,0:T(8,128)(2,1)}, u32[]{:S(2)}, u32[]{:S(2)}) async-start(bf16[128,8,768]{2,1,0:T(8,128)(2,1)} %bitcast.23), calls=%async_computation.3 | async-start | bytes 3145728 | tf_op jit(solution)/shard_map/all_to_all | solution.py:1007
  88.4 13.7 %shard_map.230 = (bf16[2048,768]{1,0:T(8,128)(2,1)}, bf16[3,2048,128]{2,1,0:T(8,128)(2,1)}, bf16[3,2048,128]{2,1,0:T(8,128)(2,1)}, bf16[256,384]{1,0:T(8,128)(2,...) custom-call(s32[3]{0:T(128)} %pad_add_fusion.place_ref, ...), custom_call_target="tpu_custom_call" | custom-call | flops 8000000000 | bytes 16777216 | tf_op jit(solution)/shard_map/pallas_call | solution.py:812
  104.5 3.9 %shard_map.231 = (f32[128,768]{1,0:T(8,128)}, bf16[128,768]{1,0:T(8,128)(2,1)}, bf16[1024,768]{1,0:T(8,128)(2,1)}) custom-call(s32[3]{0:T(128)} %pad_add_fusion.place_ref, bf16[2,128,384]{2,1,0:T(8,128)(2,1)} %get-tuple-element.50.mine_ref.att_any, bf16[2,128,384]{2,1,0:T(8,128)(2,1)} %copy-done.14, bf16[128,768]{1,0:T(8,128)(2,1)} %bitcast.189, ...), custom_call_target="tpu_custom_call" | custom-call | flops 1000000000 | bytes 16777216 | tf_op jit(solution)/shard_map/pallas_call | solution.py:812
  109.6 8.9 %all-to-all-start.2 = ((bf16[128,8,768]{2,1,0:T(8,128)(2,1)}), bf16[128,8,768]{2,1,0:T(8,128)(2,1)S(1)}, u32[]{:S(2)}, u32[]{:S(2)}) async-start(bf16[128,8,768]{2,1,0:T(8,128)(2,1)} %bitcast.190), calls=%async_computation.2 | async-start | bytes 3145728 | tf_op jit(solution)/shard_map/all_to_all | solution.py:1007
  119.9 2.2 select_reduce_fusion
  123.2 6.7 %shard_map.232.up_ref = bf16[1024,1536]{1,0:T(8,128)(2,1)} custom-call(s32[3]{0:T(128)} %pad_add_fusion.place_ref, bf16[1024,768]{1,0:T(8,128)(2,1)} %bitcast.24.cot_ref, bf16[1536,768]{1,0:T(8,128)(2,1)} %bitcast.211), custom_call_target="tpu_custom_call" | custom-call | flops 3000000000 | bytes 16777216 | tf_op jit(solution)/shard_map/pallas_call | solution.py:812
  129.9 12.0 %all-to-all-done.2 = bf16[128,8,768]{2,1,0:T(8,128)(2,1)S(1)} async-done(((bf16[128,8,768]{2,1,0:T(8,128)(2,1)}), bf16[128,8,768]{2,1,0:T(8,128)(2,1)S(1)}, u32[]{:S(2)}, u32[]{:S(2)}) %all-to-all-start.2) | async-done | bytes 1572896 | tf_op jit(solution)/shard_map/all_to_all | solution.py:1007
  143.0 13.1 %shard_map.233 = bf16[1024,1536]{1,0:T(8,128)(2,1)} custom-call(s32[3]{0:T(128)} %pad_add_fusion.place_ref, bf16[1024,768]{1,0:T(8,128)(2,1)} %bitcast.178, bf16[1024,128]{1,0:T(8,128)(2,1)} %broadcast_in_dim.87.partner_ref, bf16[1024,1536]{1,0:T(8,128)(2,1)} %shard_map.232.up_ref, bf16[768,1536]{1,0:T(8,128)(2,1)} %bitcast.213, ...), custom_call_target="tpu_custom_call" | custom-call | flops 8000000000 | bytes 20971520 | tf_op jit(solution)/shard_map/pallas_call | solution.py:941
  156.0 7.6 %all-to-all-start.4 = ((bf16[128,8,1536]{2,1,0:T(8,128)(2,1)}), bf16[128,8,1536]{2,1,0:T(8,128)(2,1)}, u32[]{:S(2)}, u32[]{:S(2)}) async-start(bf16[128,8,1536]{2,1,0:T(8,128)(2,1)} %bitcast.186), calls=%async_computation.4 | async-start | bytes 6291456 | tf_op jit(solution)/shard_map/all_to_all | solution.py:1007
  164.6 2.9 copy.125
  168.6 9.9 %shard_map.234 = (bf16[1024,1536]{1,0:T(8,128)(2,1)}, bf16[1024,1536]{1,0:T(8,128)(2,1)}) custom-call(s32[3]{0:T(128)} %pad_add_fusion.place_ref, bf16[1024,768]{1,0:T(8,128)(2,1)} %bitcast.179, bf16[1024,128]{1,0:T(8,128)(2,1)} %broadcast_in_dim.87.partner_ref, bf16[1024,1536]{1,0:T(8,128)(2,1)} %shard_map.232.up_ref, bf16[768,1536]{1,0:T(8,128)(2,1)} %bitcast.214, ...), custom_call_target="tpu_custom_call" | custom-call | flops 3000000000 | bytes 20971520 | tf_op jit(solution)/shard_map/pallas_call | solution.py:941
  178.5 7.4 %fusion.51 = f32[1536,768]{1,0:T(8,128)} fusion(bf16[1024,1536]{1,0:T(8,128)(2,1)} %get-tuple-element.56, bf16[1024,768]{1,0:T(8,128)(2,1)} %bitcast.24.cot_ref), kind=kOutput, calls=%fused_computation.139 | convolution fusion | flops 2415919104 | bytes 9437184 | tf_op jit(solution)/shard_map/dot_general | solution.py:58
  185.9 4.3 %fusion.46 = f32[768,1536]{1,0:T(8,128)} fusion(bf16[1024,1536]{1,0:T(8,128)(2,1)S(1)} %copy-done.6, bf16[128,8,768]{2,1,0:T(8,128)(2,1)S(1)} %copy-done.3), kind=kOutput, calls=%fused_computation.134 | convolution fusion | flops 2415919104 | bytes 9437184 | tf_op jit(solution)/shard_map/dot_general | solution.py:58
  190.2 13.2 %all-to-all-done.4 = bf16[128,8,1536]{2,1,0:T(8,128)(2,1)} async-done(((bf16[128,8,1536]{2,1,0:T(8,128)(2,1)}), bf16[128,8,1536]{2,1,0:T(8,128)(2,1)}, u32[]{:S(2)}, u32[]{:S(2)}) %all-to-all-start.4) | async-done | bytes 3145760 | tf_op jit(solution)/shard_map/all_to_all | solution.py:1007
  203.4 4.7 %shard_map.235 = (bf16[128,768]{1,0:T(8,128)(2,1)}, f32[128,768]{1,0:T(8,128)}, bf16[128,768]{1,0:T(8,128)(2,1)}, bf16[768,128]{1,0:T(8,128)(2,1)}) custom-call(bf16[1024,1536]{1,0:T(8,128)(2,1)} %bitcast.36.back_ref, bf16[256,1024]{1,0:T(8,128)(2,1)} %compare_convert_fusion.pick_ref, f32[128,768]{1,0:T(8,128)} %get-tuple-element.60.hidden_ref, ...), custom_call_target="tpu_custom_call" | custom-call | flops 1000000000 | bytes 16777216 | tf_op jit(solution)/shard_map/pallas_call | solution.py:812
  211.4 18.3 %shard_map.236 = (bf16[3,2048,128]{2,1,0:T(8,128)(2,1)}, bf16[3,2048,128]{2,1,0:T(8,128)(2,1)}, bf16[2,768,896]{2,1,0:T(8,128)(2,1)}, bf16[256,384]{1,0:T(8,128)(2,1)}) custom-call(s32[3]{0:T(128)} %pad_add_fusion.place_ref, bf16[256,384]{1,0:T(8,128)(2,1)} %get-tuple-element.64.q_any, bf16[3,2048,128]{2,1,0:T(8,128)(2,1)} %get-tuple-element.65.k_any, ...), custom_call_target="tpu_custom_call" | custom-call | flops 12000000000 | bytes 16777216 | tf_op jit(solution)/shard_map/pallas_call | solution.py:812
  229.7 6.0 %all-to-all-start.5 = ((bf16[64,24,896]{2,1,0:T(8,128)(2,1)}), bf16[64,24,896]{2,1,0:T(8,128)(2,1)S(1)}, u32[]{:S(2)}, u32[]{:S(2)}) async-start(bf16[64,24,896]{2,1,0:T(8,128)(2,1)} %bitcast.187), calls=%async_computation.5 | async-start | bytes 5505024 | tf_op jit(solution)/shard_map/all_to_all | solution.py:1007
  235.7 9.7 %shard_map.237 = (bf16[8,128,768]{2,1,0:T(8,128)(2,1)}, bf16[8,128,768]{2,1,0:T(8,128)(2,1)}) custom-call(s32[3]{0:T(128)} %pad_add_fusion.place_ref, bf16[256,384]{1,0:T(8,128)(2,1)} %get-tuple-element.73.dq_ref, bf16[3,2048,128]{2,1,0:T(8,128)(2,1)} %get-tuple-element.74.dk_any, bf16[3,2048,128]{2,1,0:T(8,128)(2,1)} %get-tuple-element.75.dv_any, ...), custom_call_target="tpu_custom_call" | custom-call | flops 3000000000 | bytes 16777216 | tf_op jit(solution)/shard_map/pallas_call | solution.py:812
  245.5 3.6 %collective-permute-done.7 = bf16[8,128,768]{2,1,0:T(8,128)(2,1)S(1)} collective-permute-done((bf16[8,128,768]{2,1,0:T(8,128)(2,1)}, bf16[8,128,768]{2,1,0:T(8,128)(2,1)S(1)}, u32[]{:S(2)}, u32[]{:S(2)}) %collective-permute-start.7) | collective-permute-done | bytes 1572896 | tf_op jit(solution)/shard_map/ppermute | solution.py:981
  249.1 2.9 add_convert_fusion
  252.0 23.3 %all-to-all-done.5 = bf16[64,24,896]{2,1,0:T(8,128)(2,1)S(1)} async-done(((bf16[64,24,896]{2,1,0:T(8,128)(2,1)}), bf16[64,24,896]{2,1,0:T(8,128)(2,1)S(1)}, u32[]{:S(2)}, u32[]{:S(2)}) %all-to-all-start.5) | async-done | bytes 2752544 | tf_op jit(solution)/shard_map/all_to_all | solution.py:1007
  276.0 2.0 collective-permute-start.10
  278.3 3.6 %all-to-all-start.6 = ((bf16[8,128,768]{2,1,0:T(8,128)(2,1)}), bf16[8,128,768]{2,1,0:T(8,128)(2,1)S(1)}, u32[]{:S(2)}, u32[]{:S(2)}) async-start(bf16[8,128,768]{2,1,0:T(8,128)(2,1)} %add_convert_fusion), calls=%async_computation.6 | async-start | bytes 3145728 | tf_op jit(solution)/shard_map/all_to_all | solution.py:1007
  285.6 17.2 %all-to-all-done.6 = bf16[8,128,768]{2,1,0:T(8,128)(2,1)S(1)} async-done(((bf16[8,128,768]{2,1,0:T(8,128)(2,1)}), bf16[8,128,768]{2,1,0:T(8,128)(2,1)S(1)}, u32[]{:S(2)}, u32[]{:S(2)}) %all-to-all-start.6) | async-done | bytes 1572896 | tf_op jit(solution)/shard_map/all_to_all | solution.py:1007
  (177 shorter events, 28.7 us)
Async XLA Ops:
  0.6 42.4 %copy-start = (f32[32,12]{0,1:T(8,128)S(1)}, f32[32,12]{0,1:T(8,128)}, u32[]{:S(2)}) copy-start(f32[32,12]{0,1:T(8,128)} %param.24) | copy-start | bytes 4612
  0.7 10.5 %copy-start.18 = (bf16[6,768]{1,0:T(8,128)(2,1)S(1)}, bf16[6,768]{1,0:T(8,128)(2,1)}, u32[]{:S(2)}) copy-start(bf16[6,768]{1,0:T(8,128)(2,1)} %param.19) | copy-start | bytes 27652
  0.7 10.5 %copy-start.20 = (bf16[6,768]{1,0:T(8,128)(2,1)S(1)}, bf16[6,768]{1,0:T(8,128)(2,1)}, u32[]{:S(2)}) copy-start(bf16[6,768]{1,0:T(8,128)(2,1)} %param.18) | copy-start | bytes 27652
  0.7 10.6 %copy-start.22 = (bf16[6,768]{1,0:T(8,128)(2,1)S(1)}, bf16[6,768]{1,0:T(8,128)(2,1)}, u32[]{:S(2)}) copy-start(bf16[6,768]{1,0:T(8,128)(2,1)} %param.17) | copy-start | bytes 27652
  0.7 10.7 %copy-start.28 = (bf16[6]{0:T(256)(128)(2,1)S(1)}, bf16[6]{0:T(256)(128)(2,1)}, u32[]{:S(2)}) copy-start(bf16[6]{0:T(256)(128)(2,1)} %param.23) | copy-start | bytes 40
  0.7 10.8 %copy-start.29 = (bf16[6]{0:T(256)(128)(2,1)S(1)}, bf16[6]{0:T(256)(128)(2,1)}, u32[]{:S(2)}) copy-start(bf16[6]{0:T(256)(128)(2,1)} %param.22) | copy-start | bytes 40
  0.7 11.0 %copy-start.26 = (bf16[6,64]{1,0:T(8,128)(2,1)S(1)}, bf16[6,64]{1,0:T(8,128)(2,1)}, u32[]{:S(2)}) copy-start(bf16[6,64]{1,0:T(8,128)(2,1)} %param.21) | copy-start | bytes 2308
  3.0 29.0 %all-to-all-start = ((bf16[8,128,768]{2,1,0:T(8,128)(2,1)}), bf16[8,128,768]{2,1,0:T(8,128)(2,1)S(1)}, u32[]{:S(2)}, u32[]{:S(2)}) async-start(bf16[8,128,768]{2,1,0:T(8,128)(2,1)} %broadcast_in_dim.77), calls=%async_computation | async-start | bytes 3145728 | tf_op jit(solution)/shard_map/all_to_all | solution.py:986
  11.0 34.0 %copy-start.9 = (s32[1,128,2]{2,1,0:T(8,128)}, s32[1,128,2]{2,1,0:T(8,128)S(1)}, u32[]{:S(2)}) copy-start(s32[1,128,2]{2,1,0:T(8,128)S(1)} %copy.105) | copy-start | bytes 3076
  12.0 16.4 %collective-permute-start.1 = (bf16[6,896]{1,0:T(8,128)(2,1)S(1)}, bf16[6,896]{1,0:T(8,128)(2,1)S(1)}, u32[]{:S(2)}, u32[]{:S(2)}) collective-permute-start(bf16[6,896]{1,0:T(8,128)(2,1)S(1)} %bitcast.205), channel_id=1, source_target_pairs={{0,3},{1,2},{2,1},{3,0},{4,7},{5,6},{6,5},{7,4},{8,11},{9,10},{10,... | collective-permute-start | bytes 32264 | tf_op jit(solution)/shard_map/ppermute | solution.py:996
  12.1 16.3 %collective-permute-start.2 = (bf16[6,896]{1,0:T(8,128)(2,1)S(1)}, bf16[6,896]{1,0:T(8,128)(2,1)S(1)}, u32[]{:S(2)}, u32[]{:S(2)}) collective-permute-start(bf16[6,896]{1,0:T(8,128)(2,1)S(1)} %bitcast.206), channel_id=1, source_target_pairs={{0,2},{1,3},{2,0},{3,1},{4,6},{5,7},{6,4},{7,5},{8,10},{9,11},{10,... | collective-permute-start | bytes 32264 | tf_op jit(solution)/shard_map/ppermute | solution.py:996
  12.9 16.8 %collective-permute-start.3 = (bf16[6,896]{1,0:T(8,128)(2,1)S(1)}, bf16[6,896]{1,0:T(8,128)(2,1)S(1)}, u32[]{:S(2)}, u32[]{:S(2)}) collective-permute-start(bf16[6,896]{1,0:T(8,128)(2,1)S(1)} %bitcast.207), channel_id=1, source_target_pairs={{0,1},{1,0},{2,3},{3,2},{4,5},{5,4},{6,7},{7,6},{8,9},{9,8},{10,11... | collective-permute-start | bytes 32264 | tf_op jit(solution)/shard_map/ppermute | solution.py:996
  34.0 44.0 %all-to-all-start.1 = ((bf16[64,24,896]{2,1,0:T(8,128)(2,1)}), bf16[64,24,896]{2,1,0:T(8,128)(2,1)S(1)}, u32[]{:S(2)}, u32[]{:S(2)}) async-start(bf16[64,24,896]{2,1,0:T(8,128)(2,1)} %broadcast_in_dim.83), calls=%async_computation.1 | async-start | bytes 5505024 | tf_op jit(solution)/shard_map/all_to_all | solution.py:986
  43.0 35.0 %collective-permute-start = (bf16[8,128,768]{2,1,0:T(8,128)(2,1)}, bf16[8,128,768]{2,1,0:T(8,128)(2,1)}, u32[]{:S(2)}, u32[]{:S(2)}) collective-permute-start(bf16[8,128,768]{2,1,0:T(8,128)(2,1)} %copy-done.8), channel_id=1, source_target_pairs={{0,2},{2,0},{1,3},{3,1},{4,6},{6,4},{5,7},{7,5},{8,10},{10,8},{9,1... | collective-permute-start | bytes 4718600 | tf_op jit(solution)/shard_map/ppermute | solution.py:981
  48.3 39.8 %copy-start.10 = (bf16[1024,128]{1,0:T(8,128)(2,1)}, bf16[1024,128]{1,0:T(8,128)(2,1)S(1)}, u32[]{:S(2)}) copy-start(bf16[1024,128]{1,0:T(8,128)(2,1)S(1)} %fusion.6.pack_ref) | copy-start | bytes 786436
  78.0 31.6 %all-to-all-start.3 = ((bf16[128,8,768]{2,1,0:T(8,128)(2,1)}), bf16[128,8,768]{2,1,0:T(8,128)(2,1)}, u32[]{:S(2)}, u32[]{:S(2)}) async-start(bf16[128,8,768]{2,1,0:T(8,128)(2,1)} %bitcast.23), calls=%async_computation.3 | async-start | bytes 3145728 | tf_op jit(solution)/shard_map/all_to_all | solution.py:1007
  88.1 15.7 %collective-permute-start.5 = (bf16[768,384]{1,0:T(8,128)(2,1)}, bf16[768,384]{1,0:T(8,128)(2,1)}, u32[]{:S(2)}, u32[]{:S(2)}) collective-permute-start(bf16[768,384]{1,0:T(8,128)(2,1)} %slice_bitcast_fusion.wo_mine_ref.wo_mine_any), channel_id=1, source_target_pairs={{0,2},{2,0},{1,3},{3,1},{4,6},{6,4},{5,7},{7,5},{8,10},{10,8},{9,1... | collective-permute-start | bytes 1769480 | tf_op jit(solution)/shard_map/ppermute | solution.py:981
  102.1 1.7 collective-permute-start.4
  109.6 32.2 %all-to-all-start.2 = ((bf16[128,8,768]{2,1,0:T(8,128)(2,1)}), bf16[128,8,768]{2,1,0:T(8,128)(2,1)S(1)}, u32[]{:S(2)}, u32[]{:S(2)}) async-start(bf16[128,8,768]{2,1,0:T(8,128)(2,1)} %bitcast.190), calls=%async_computation.2 | async-start | bytes 3145728 | tf_op jit(solution)/shard_map/all_to_all | solution.py:1007
  156.0 47.4 %all-to-all-start.4 = ((bf16[128,8,1536]{2,1,0:T(8,128)(2,1)}), bf16[128,8,1536]{2,1,0:T(8,128)(2,1)}, u32[]{:S(2)}, u32[]{:S(2)}) async-start(bf16[128,8,1536]{2,1,0:T(8,128)(2,1)} %bitcast.186), calls=%async_computation.4 | async-start | bytes 6291456 | tf_op jit(solution)/shard_map/all_to_all | solution.py:1007
  208.1 2.6 collective-permute-start.6
  229.7 45.6 %all-to-all-start.5 = ((bf16[64,24,896]{2,1,0:T(8,128)(2,1)}), bf16[64,24,896]{2,1,0:T(8,128)(2,1)S(1)}, u32[]{:S(2)}, u32[]{:S(2)}) async-start(bf16[64,24,896]{2,1,0:T(8,128)(2,1)} %bitcast.187), calls=%async_computation.5 | async-start | bytes 5505024 | tf_op jit(solution)/shard_map/all_to_all | solution.py:1007
  245.4 3.7 %collective-permute-start.7 = (bf16[8,128,768]{2,1,0:T(8,128)(2,1)}, bf16[8,128,768]{2,1,0:T(8,128)(2,1)S(1)}, u32[]{:S(2)}, u32[]{:S(2)}) collective-permute-start(bf16[8,128,768]{2,1,0:T(8,128)(2,1)} %get-tuple-element.77), channel_id=1, source_target_pairs={{0,2},{2,0},{1,3},{3,1},{4,6},{6,4},{5,7},{7,5},{8,10},{10,8},{9,1... | collective-permute-start | bytes 4718600 | tf_op jit(solution)/shard_map/ppermute | solution.py:981
  252.0 26.1 %copy-start.12 = (bf16[768,128]{1,0:T(8,128)(2,1)S(1)}, bf16[768,128]{1,0:T(8,128)(2,1)}, u32[]{:S(2)}) copy-start(bf16[768,128]{1,0:T(8,128)(2,1)} %get-tuple-element.51.side_ref) | copy-start | bytes 589828
  275.8 6.1 %collective-permute-start.8 = (f32[10,896]{1,0:T(8,128)S(1)}, f32[10,896]{1,0:T(8,128)S(1)}, u32[]{:S(2)}, u32[]{:S(2)}) collective-permute-start(f32[10,896]{1,0:T(8,128)S(1)} %get-tuple-element.104), channel_id=1, source_target_pairs={{0,3},{1,2},{2,1},{3,0},{4,7},{5,6},{6,5},{7,4},{8,11},{9,10},{10,... | collective-permute-start | bytes 107528 | tf_op jit(solution)/shard_map/ppermute | solution.py:996
  275.9 6.0 %collective-permute-start.9 = (f32[10,896]{1,0:T(8,128)S(1)}, f32[10,896]{1,0:T(8,128)S(1)}, u32[]{:S(2)}, u32[]{:S(2)}) collective-permute-start(f32[10,896]{1,0:T(8,128)S(1)} %get-tuple-element.105), channel_id=1, source_target_pairs={{0,2},{1,3},{2,0},{3,1},{4,6},{5,7},{6,4},{7,5},{8,10},{9,11},{10,... | collective-permute-start | bytes 107528 | tf_op jit(solution)/shard_map/ppermute | solution.py:996
  276.0 5.9 %collective-permute-start.10 = (f32[10,896]{1,0:T(8,128)S(1)}, f32[10,896]{1,0:T(8,128)S(1)}, u32[]{:S(2)}, u32[]{:S(2)}) collective-permute-start(f32[10,896]{1,0:T(8,128)S(1)} %get-tuple-element.103), channel_id=1, source_target_pairs={{0,1},{1,0},{2,3},{3,2},{4,5},{5,4},{6,7},{7,6},{8,9},{9,8},{10,11... | collective-permute-start | bytes 107528 | tf_op jit(solution)/shard_map/ppermute | solution.py:996
  278.3 24.5 %all-to-all-start.6 = ((bf16[8,128,768]{2,1,0:T(8,128)(2,1)}), bf16[8,128,768]{2,1,0:T(8,128)(2,1)S(1)}, u32[]{:S(2)}, u32[]{:S(2)}) async-start(bf16[8,128,768]{2,1,0:T(8,128)(2,1)} %add_convert_fusion), calls=%async_computation.6 | async-start | bytes 3145728 | tf_op jit(solution)/shard_map/all_to_all | solution.py:1007
  281.9 21.1 %copy-start.7 = (bf16[1,128,768]{2,1,0:T(8,128)(2,1)S(1)}, bf16[1,128,768]{2,1,0:T(8,128)(2,1)}, u32[]{:S(2)}) copy-start(bf16[1,128,768]{2,1,0:T(8,128)(2,1)} %param.14) | copy-start | bytes 589828
  281.9 21.3 %copy-start.11 = (f32[128,768]{1,0:T(8,128)S(1)}, f32[128,768]{1,0:T(8,128)}, u32[]{:S(2)}) copy-start(f32[128,768]{1,0:T(8,128)} %get-tuple-element.63) | copy-start | bytes 1179652
  282.0 22.2 %copy-start.1 = (f32[32,12]{0,1:T(8,128)S(1)}, f32[32,12]{0,1:T(8,128)}, u32[]{:S(2)}) copy-start(f32[32,12]{0,1:T(8,128)} %param.24) | copy-start | bytes 4612
  282.2 21.9 %copy-start.24 = (f32[6,128]{1,0:T(8,128)}, f32[6,128]{1,0:T(8,128)S(1)}, u32[]{:S(2)}) copy-start(f32[6,128]{1,0:T(8,128)S(1)} %fusion.43) | copy-start | bytes 9220
  (17 other events, 100.3 us)
